TPU v7x, 256 devices: a whole 4x4x8 slice. The times are simulated.
256 devices in a mesh: dp: 16 (over z, core), seq: 4 (over y), vocab: 4 (over x).
Axes of the slice: x: 4, y: 4, z: 8, core: 2. Of those that a mesh axis runs over, the one named last changes fastest.
Arguments:
- hidden: bfloat16 [1024, 4096], P(('dp', 'vocab'), 'seq'), may hold values from -40 to 40
- head_weight: bfloat16 [4096, 81920], P('seq', ('dp', 'vocab')), may hold values from -1 to 1
- targets: int32 [1024], replicated, may hold values from 0 to 81919
- weights: float32 [1024], replicated, may hold values from -4 to 4
Outputs:
- log_prob: float32 [1024], P('seq')
- hidden_grad: bfloat16 [1024, 4096], P(('dp', 'vocab'), 'seq')
- head_grad: bfloat16 [4096, 81920], P('seq', ('dp', 'vocab'))
All inputs are finite; a program needn't handle non-finite values.
Results may differ from a plain program's by a relative error of at most 0.0047.
Values may be sent and summed in bfloat16 or wider, within the bound.
No kernel may reach another device: no remote copies, remote signals or barrier semaphores. Data moves between devices by JAX's collectives and lax.ppermute only.
A program may use at most 64 MiB of HBM per device.

v0:
```python
import jax
import jax.numpy as jnp
from jax import lax
from jax.sharding import PartitionSpec as P


def body(hidden, head_weight, targets, weights):
    gathered = lax.all_gather(hidden, ("dp", "vocab"), axis=0, tiled=True)
    tokens = gathered.shape[0]
    columns = head_weight.shape[1]
    block_rows = tokens // lax.axis_size("seq")
    seq_start = lax.axis_index("seq") * block_rows
    column_ids = lax.axis_index(("dp", "vocab")) * columns + jnp.arange(columns, dtype=jnp.int32)
    partial_logits = jnp.dot(gathered, head_weight, preferred_element_type=jnp.float32)
    logits = lax.psum(partial_logits, "seq")
    is_target = column_ids[None, :] == targets[:, None]
    picked_part = jnp.sum(jnp.where(is_target, logits, jnp.zeros_like(logits)), axis=1)
    row_max = lax.pmax(jnp.max(logits, axis=1), ("dp", "vocab"))
    exp_part = jnp.sum(jnp.exp(logits - row_max[:, None]), axis=1)
    sum_total, picked = lax.psum((exp_part, picked_part), ("dp", "vocab"))
    log_total = row_max + jnp.log(sum_total)
    log_prob = picked - log_total
    softmax_rows = jnp.exp(logits - log_total[:, None])
    logit_grad = (weights[:, None] * (is_target.astype(jnp.float32) - softmax_rows)).astype(
        jnp.bfloat16
    )
    log_prob = lax.dynamic_slice_in_dim(log_prob, seq_start, block_rows, 0)
    head_grad = lax.dot_general(
        gathered, logit_grad, (((0,), (0,)), ((), ())), preferred_element_type=jnp.float32
    ).astype(jnp.bfloat16)
    hidden_grad = lax.psum_scatter(
        lax.dot_general(
            logit_grad, head_weight, (((1,), (1,)), ((), ())), preferred_element_type=jnp.float32
        ),
        ("dp", "vocab"),
        scatter_dimension=0,
        tiled=True,
    ).astype(jnp.bfloat16)
    return (log_prob, hidden_grad, head_grad)


def solution(mesh):
    placed = (P(("dp", "vocab"), "seq"), P("seq", ("dp", "vocab")), P(), P())
    return jax.shard_map(
        body,
        mesh=mesh,
        in_specs=placed,
        out_specs=(P("seq"), P(("dp", "vocab"), "seq"), P("seq", ("dp", "vocab"))),
        check_vma=False,
    )
```

profile of v0, /device:TPU:6, one launch (start us, length us, event | category | flops | bytes accessed | tf_op | source)
XLA Modules:
  0.0 629.0 jit_solution(7617942346546642913)
XLA Ops:
  7.2 0.0 copy-start
  7.2 0.0 all-gather.2.cloned.1.call-start
  7.2 0.7 all-gather.2.cloned.1.call-update
  7.9 0.0 all-reduce.3.cloned.1.call-start
  8.0 82.0 %all-gather.2.cloned.1.call-done = bf16[1024,1024]{1,0:T(8,128)(2,1)} async-done(((bf16[16,1024]{1,0:T(8,128)(2,1)}), bf16[1024,1024]{1,0:T(8,128)(2,1)}) %all-gather.2.cloned.1.call-update) | async-done | bytes 2097168 | tf_op jit(solution)/shard_map/all_gather | solution.py:8
  89.9 0.0 copy-done
  89.9 6.8 %fusion.6 = f32[1024,1280]{1,0:T(8,128)} fusion(bf16[1024,1024]{1,0:T(8,128)(2,1)} %all-gather.2.cloned.1.call-done, bf16[1024,1280]{1,0:T(8,128)(2,1)S(1)} %copy-done), kind=kOutput, calls=%fused_computation.12 | convolution fusion | flops 2684354560 | bytes 9961472 | tf_op jit(solution)/shard_map/dot_general | solution.py:14
  96.8 0.0 all-reduce.3.cloned.1.call-update
  96.8 0.0 reduce-scatter.2.cloned.1.call-start
  96.9 0.0 copy-start.2
  96.9 113.7 %all-reduce.3.cloned.1.call-done = f32[1024,1280]{1,0:T(8,128)} async-done(((f32[1024,1280]{1,0:T(8,128)}), f32[1024,1280]{1,0:T(8,128)}) %all-reduce.3.cloned.1.call-update) | async-done | bytes 5242896 | tf_op jit(solution)/shard_map/psum | solution.py:15
  210.6 2.8 reduce_max.9
  213.4 122.2 %pmax.7 = f32[1024]{0:T(1024)S(1)} all-reduce(f32[1024]{0:T(1024)S(1)} %reduce_max.9), channel_id=1, replica_groups=mesh['dp'=16,'seq'=4,'vocab'=4] {'dp','vocab'}, use_global_device_ids=true, to_apply=%region_4.5 | all-reduce | flops 1024 | bytes 8192 | tf_op jit(solution)/shard_map/pmax | solution.py:18
  335.5 0.0 copy-done.2
  335.6 0.0 copy-start.3
  335.6 3.4 exponential_reduce_fusion
  338.9 130.8 %all-reduce = (f32[1024]{0:T(1024)S(1)}, f32[1024]{0:T(1024)S(1)}) all-reduce(f32[1024]{0:T(1024)S(1)} %get-tuple-element.7, f32[1024]{0:T(1024)S(1)} %get-tuple-element.6), channel_id=1, replica_groups=mesh['dp'=16,'seq'=4,'vocab'=4] {'dp','vocab'}, use_global_device_ids=true, to_apply=%region_2.3 | all-reduce | flops 2048 | bytes 16384 | tf_op jit(solution)/shard_map/psum | solution.py:20
  469.7 0.0 copy-done.3
  469.8 3.3 fusion.3
  473.1 0.0 copy-start.1
  473.1 1.5 copy-done.1
  474.6 4.5 fusion.7
  479.0 0.0 reduce-scatter.2.cloned.1.call-update
  479.1 6.8 %fusion.4 = bf16[1024,1280]{0,1:T(8,128)(2,1)} fusion(bf16[1024,1280]{1,0:T(8,128)(2,1)} %copy-done.1, bf16[1024,1024]{1,0:T(8,128)(2,1)} %all-gather.2.cloned.1.call-done), kind=kOutput, calls=%fused_computation.8 | convolution fusion | flops 2685665280 | bytes 7340032 | tf_op jit(solution)/shard_map/dot_general | solution.py:28
  485.9 4.4 copy.7
  490.3 0.6 dynamic_slice.3
  490.9 130.0 %reduce-scatter.2.cloned.1.call-done = f32[16,1024]{1,0:T(8,128)} async-done(((f32[1024,1024]{1,0:T(8,128)}), f32[16,1024]{1,0:T(8,128)}) %reduce-scatter.2.cloned.1.call-update) | async-done | bytes 65552 | tf_op jit(solution)/shard_map/reduce_scatter | solution.py:31
  621.0 1.5 convert_element_type.17
  (2 shorter events, 0.0 us)
Async XLA Ops:
  7.2 82.8 %copy-start = (bf16[1024,1280]{1,0:T(8,128)(2,1)S(1)}, bf16[1024,1280]{1,0:T(8,128)(2,1)}, u32[]{:S(2)}) copy-start(bf16[1024,1280]{1,0:T(8,128)(2,1)} %param.5) | copy-start | bytes 7864324
  7.2 82.8 %all-gather.2.cloned.1.call-start = ((), (), s32[]{:S(2)}) async-start(), calls=%async_computation.1 | async-start | bytes 2129920 | tf_op jit(solution)/shard_map/all_gather | solution.py:8
  7.9 202.7 %all-reduce.3.cloned.1.call-start = ((), (), s32[]{:S(2)}) async-start(), calls=%async_computation.2 | async-start | bytes 10485760 | tf_op jit(solution)/shard_map/psum | solution.py:15
  96.8 524.2 %reduce-scatter.2.cloned.1.call-start = ((), (), s32[]{:S(2)}) async-start(), calls=%async_computation.3 | async-start | bytes 4259840 | tf_op jit(solution)/shard_map/reduce_scatter | solution.py:31
  96.9 238.7 %copy-start.2 = (s32[1024]{0:T(1024)S(1)}, s32[1024]{0:T(1024)}, u32[]{:S(2)}) copy-start(s32[1024]{0:T(1024)} %param.6) | copy-start | bytes 12292
  335.6 134.2 %copy-start.3 = (f32[1024]{0:T(1024)S(1)}, f32[1024]{0:T(1024)}, u32[]{:S(2)}) copy-start(f32[1024]{0:T(1024)} %param.7) | copy-start | bytes 12292
  473.1 1.5 copy-start.1
Sparse Core Ops, SparseCore 0:
  10.8 79.1 all-gather.1
  96.9 113.6 all-reduce.2
  479.2 141.7 reduce-scatter.1
where the time goes:
time: 630 us; the launch traced here: 629 us
  waiting for transfers between devices  326 us (52%)
  blocking collectives  253 us (40%)
  matrix products  18.1 us (3%)
  between operations  13.8 us (2%)
  other arithmetic  10.9 us (2%)
  local copies, waits for them, and re-layouts  6.53 us (1%)
    psum x1, blocking collectives, body(): sum_total, picked = lax.psum((exp_part, picked_part), ('dp', 'vocab'))  131 us
    reduce_scatter x1, waiting for transfers between devices, body(): lax.psum_scatter(lax.dot_general(logit_grad, head_weight, (((1,), (1,)),...  130 us
    pmax x1, blocking collectives, body(): row_max = lax.pmax(jnp.max(logits, axis=1), ('dp', 'vocab'))  122 us
    psum x1, waiting for transfers between devices, body(): logits = lax.psum(partial_logits, 'seq')  114 us
    all_gather x1, waiting for transfers between devices, body(): gathered = lax.all_gather(hidden, ('dp', 'vocab'), axis=0, tiled=True)  82 us
  transfers between devices with their start and end apart: 3, of which 3 were waited for; matrix products, arithmetic and copies ran while one was open for 2% of the time, Pallas kernels for 0%

commit v1 on v0

v1 whole, which is shorter than its diff:
```python
import jax
import jax.numpy as jnp
from jax import lax
from jax.experimental import pallas as pl
from jax.experimental.pallas import tpu as pltpu
from jax.sharding import Mesh, PartitionSpec as P

F32 = jnp.float32
BF16 = jnp.bfloat16
NZ, NC, NY, NX = 8, 2, 4, 4
VMEM = pl.BlockSpec(memory_space=pltpu.VMEM)
SMEM = pl.BlockSpec(memory_space=pltpu.SMEM)


def shift(n, d):
    return [(i, (i + d) % n) for i in range(n)]


SWAP = [(0, 1), (1, 0)]


ANY = pl.BlockSpec(memory_space=pl.ANY)


def call(kernel, outs, args, scratch=(), flops=1000, moved=1000, far=0):
    return pl.pallas_call(
        kernel,
        out_shape=[jax.ShapeDtypeStruct(s, d) for s, d in outs],
        in_specs=[SMEM] + [VMEM] * (len(args) - 1 - far) + [ANY] * far,
        out_specs=[VMEM] * len(outs),
        scratch_shapes=list(scratch),
        cost_estimate=pl.CostEstimate(flops=flops, bytes_accessed=moved, transcendentals=0),
        compiler_params=pltpu.CompilerParams(vmem_limit_bytes=24 * 2**20),
    )(*args)


def logits_kernel(pos, targets, b0, b1, b2, b3, hid, *refs):
    e_out, stats_out, slice_out, acc, hid_v, sems = refs
    z, c, y, x = (pos[i] for i in range(4))
    width, group = b0.shape
    rows = e_out.shape[0]
    copies = []
    for i in range(4):
        core = c if i < 2 else 1 - c
        origin = 2 * core + lax.rem(y + i, 2)
        cols = pl.ds(pl.multiple_of(origin * width, 128), width)
        copies.append(pltpu.make_async_copy(hid.at[:, cols], hid_v.at[i], sems.at[i]))
    for copy in copies:
        copy.start()
    for i, block in enumerate((b0, b1, b2, b3)):
        copies[i].wait()
        term = jnp.dot(hid_v[i], block[...], preferred_element_type=F32)
        acc[...] = term if i == 0 else acc[...] + term

        @pl.when((c if i < 2 else 1 - c) * 2 + lax.rem(y + i, 2) == y)
        def _():
            slice_out[...] = hid_v[i]

    logits = acc[...]
    top = jnp.max(logits, axis=1, keepdims=True)
    e = jnp.exp(logits - top)
    total = jnp.sum(e, axis=1, keepdims=True)
    first = ((z * NC + y // 2) * NX + x) * (2 * group) + lax.rem(y, 2) * group
    ids = first + lax.broadcasted_iota(jnp.int32, (rows, group), 1)
    picked = jnp.sum(jnp.where(ids == targets[...], logits, 0.0), axis=1, keepdims=True)
    e_out[...] = e.astype(BF16)
    lane = lax.broadcasted_iota(jnp.int32, (rows, 128), 1)
    table = jnp.where(lane == 0, top, jnp.where(lane == 1, total, jnp.where(lane == 2, picked, 0.0)))
    flat = table.T
    packed = pack([flat[0:1], flat[1:2], flat[2:3]])
    for i in range(stats_out.shape[0]):
        stats_out[i] = packed


def pack(vectors):
    parts = [v[:, i : i + 128] for v in vectors for i in range(0, v.shape[1], 128)]
    return jnp.concatenate(parts + [jnp.zeros((16 - len(parts), 128), F32)], axis=0)


def unpack(tiles):
    return jnp.concatenate([tiles[i : i + 1] for i in range(tiles.shape[0])], axis=1)


def merged(table):
    m, s, p = table[:, 0:4], table[:, 4:8], table[:, 8:12]
    top = jnp.max(m, axis=0)
    return top, jnp.sum(s * jnp.exp(m - top[None]), axis=0), jnp.sum(p, axis=0)


def near_kernel(pos, got, out):
    m, s, p = merged(got[...])
    packed = jnp.concatenate([m, s, p, jnp.zeros_like(m)], axis=0)
    for i in range(out.shape[0]):
        out[i] = packed


def far_kernel(pos, far, near, weights, vec_out, log_prob_out):
    y = pos[2]
    m, s, p = (unpack(v) for v in merged(far[...]))
    log_total = m + jnp.log(s)
    log_prob = p - log_total
    w = weights[...]
    rows = []
    for d in range(NY):
        local = unpack(near[lax.rem(y + NY - d, NY)][0:4])
        rows.append(-w * jnp.exp(local - log_total))
    rows.append(w * (1.0 - jnp.exp(log_prob)))
    rows.append(jnp.zeros((3, m.shape[1]), F32))
    vec_out[...] = jnp.concatenate(rows, axis=0)
    log_prob_out[...] = jnp.broadcast_to(log_prob, log_prob_out.shape)


def grad_kernel(pos, targets, vec, e0, e1, e2, e3, own, other, g0, g1, keep, s1, s2, s3, part):
    z, c, y, x = (pos[i] for i in range(4))
    rows, group = e0.shape
    cols = jnp.concatenate([vec[...], jnp.zeros((120, rows), F32)], axis=0).T
    t = targets[...]
    for d, e in enumerate((e0, e1, e2, e3)):
        g = lax.rem(y + NY - d, NY)
        first = ((z * NC + g // 2) * NX + x) * (2 * group) + lax.rem(g, 2) * group
        ids = first + lax.broadcasted_iota(jnp.int32, (rows, group), 1)
        value = jnp.where(ids == t, cols[:, 4:5], e[...].astype(F32) * cols[:, d : d + 1])
        value = value.astype(BF16)
        at = pl.ds(pl.multiple_of(lax.rem(g, 2) * group, 128), group)
        same = g // 2 == c

        @pl.when(same)
        def _():
            g0[:, at] = value

        @pl.when(jnp.logical_not(same))
        def _():
            g1[:, at] = value

    nt = (((1,), (1,)), ((), ()))
    sums = lax.dot_general(g0[...], own[...], nt, preferred_element_type=F32)
    sums += lax.dot_general(g1[...], other[...], nt, preferred_element_type=F32)
    part[...] = sums.reshape(part.shape)
    keep[...] = part[:, x]
    for d, out in enumerate((s1, s2, s3)):
        out[...] = part[:, lax.rem(x + d + 1, NX)].astype(BF16)


def head_kernel(pos, h0, h1, g0, g1, out):
    tn = (((0,), (0,)), ((), ()))
    step = 256
    for i in range(0, out.shape[0], step):
        total = lax.dot_general(h0[:, i : i + step], g0[...], tn, preferred_element_type=F32)
        total += lax.dot_general(h1[:, i : i + step], g1[...], tn, preferred_element_type=F32)
        out[i : i + step] = total.astype(BF16)


def tie(*arrays):
    return lax.optimization_barrier(arrays)


def body(hidden, head, targets, weights):
    rows, width = hidden.shape
    columns = head.shape[1]
    group = columns // 2
    half = width // 2
    per_z = NX * rows
    z, c, y, x = (lax.axis_index(a) for a in ("z", "core", "y", "x"))
    pos = jnp.stack([z, c, y, x]).astype(jnp.int32)

    def copies(v, n, axis):
        flat = jnp.broadcast_to(v[None], (n,) + v.shape).reshape((n * v.shape[0],) + v.shape[1:])
        return lax.all_to_all(flat, axis, 0, 0, tiled=True).reshape((n,) + v.shape)

    near = copies(hidden, NY, "y")
    def block(k):
        return lax.dynamic_slice_in_dim(head, ((y + k) % 2) * group, group, 1)

    def hand_over(v, k):
        perm = [
            (i * NY + j, (j // 2) * NY + 2 * i + (j + k) % 2) for i in range(NC) for j in range(NY)
        ]
        return lax.ppermute(v, ("core", "y"), perm)

    near, block0, block1 = tie(near, block(0), block(1))
    got0, got1 = hand_over(block0, 0), hand_over(block1, 1)
    near = near.transpose(1, 0, 2).reshape(rows, NY * width)
    near = copies(near, NX, "x").reshape(per_z, NY * width)

    def ordered(v):
        v = lax.dynamic_index_in_dim(v.reshape(NZ, NC, per_z), c, 1, False)
        return v.reshape(NZ * per_z)

    my_targets, my_weights = ordered(targets)[:, None], ordered(weights)[None]

    hid = lax.all_gather(near, "z", axis=0, tiled=True)
    twin0, twin1 = lax.ppermute(got0, "core", SWAP), lax.ppermute(got1, "core", SWAP)
    twin0, twin1, head_later = tie(twin0, twin1, head)
    other = lax.ppermute(head_later, "core", SWAP)

    size = NZ * per_z
    e, stats, mine = call(
        logits_kernel,
        [((size, group), BF16), ((NY, 16, 128), F32), ((size, width), BF16)],
        (pos, my_targets, got0, got1, twin0, twin1, hid),
        scratch=[
            pltpu.VMEM((size, group), F32),
            pltpu.VMEM((NY, size, width), BF16),
            pltpu.SemaphoreType.DMA((NY,)),
        ],
        far=1,
    )

    close = lax.all_to_all(stats, "y", 0, 0, tiled=True)
    close, e, mine = tie(close, e, mine)
    exps = [e] + [lax.ppermute(e, "y", shift(NY, d)) for d in (2, 1, 3)]
    exps = [exps[0], exps[2], exps[1], exps[3]]
    (wide,) = call(near_kernel, [((NZ * NX, 16, 128), F32)], (pos, close))
    far = lax.all_to_all(wide, ("z", "x"), 0, 0, tiled=True)
    vec, lp = call(
        far_kernel, [((8, size), F32), ((8, size), F32)], (pos, far, close, my_weights)
    )
    twin_mine = lax.ppermute(mine, "core", SWAP)

    kept, sent, keep, *send = call(
        grad_kernel,
        [((size, columns), BF16)] * 2
        + [((NZ, rows, width), F32)]
        + [((NZ, rows, width), BF16)] * 3,
        (pos, my_targets, vec, *exps, head, other),
        scratch=[pltpu.VMEM((NZ, NX, rows, width), F32)],
    )
    for d, v in enumerate(send):
        keep = keep + lax.ppermute(v, "x", shift(NX, d + 1)).astype(F32)
    twin_kept = lax.ppermute(sent, "core", SWAP)
    keep, twin_kept, twin_mine = tie(keep, twin_kept, twin_mine)

    total = keep.astype(BF16).reshape(NZ * rows, width)
    got = lax.all_to_all(total, "z", 0, 0, tiled=True)
    (head_grad,) = call(
        head_kernel,
        [((width, columns), BF16)],
        (pos, mine, twin_mine, kept, twin_kept),
        flops=2 * NZ * NC * per_z * columns * width,
        moved=8 * 2**20,
    )
    hidden_grad = jnp.sum(got.reshape(NZ, rows, width).astype(F32), axis=0).astype(BF16)

    log_prob = lp[0]
    own = lax.dynamic_slice_in_dim(log_prob, 2 * y * per_z, 2 * per_z, 0)
    oth = lax.ppermute(own, "core", SWAP)
    pairs = jnp.where(c == 0, jnp.stack([own, oth]), jnp.stack([oth, own]))
    log_prob_out = pairs.reshape(NC, 2, per_z).transpose(1, 0, 2).reshape(-1)
    return log_prob_out, hidden_grad, head_grad


def solution(mesh):
    fine = Mesh(mesh.devices.reshape(NZ, NC, NY, NX), ("z", "core", "y", "x"))
    tok = ("z", "core", "x")
    return jax.shard_map(
        body,
        mesh=fine,
        in_specs=(P(tok, "y"), P("y", tok), P(), P()),
        out_specs=(P("y"), P(tok, "y"), P("y", tok)),
        check_vma=False,
    )
```

time: 630 us -> 193 us (0.31)
  waiting for transfers between devices: 326 us -> 52 us
  blocking collectives: 253 us -> 20.2 us
  starting transfers between devices: 0.12 us -> 59.6 us
  Pallas kernels: 0 us -> 22 us
  matrix products: 18.1 us -> 0 us
  local copies, waits for them, and re-layouts: 6.53 us -> 22.7 us
  other arithmetic: 10.9 us -> 1.59 us
    psum x1 -> x0, blocking collectives: 131 us -> none  [body(): sum_total, picked = lax.psum((exp_part, picked_part), ('dp', 'vocab'))]
    reduce_scatter x1 -> x0, waiting for transfers between devices: 130 us -> none  [body(): lax.psum_scatter(lax.dot_general(logit_grad, head_weight, (((1,), (1,)),...]
    pmax x1 -> x0, blocking collectives: 122 us -> none  [body(): row_max = lax.pmax(jnp.max(logits, axis=1), ('dp', 'vocab'))]
    psum x1 -> x0, waiting for transfers between devices: 114 us -> none  [body(): logits = lax.psum(partial_logits, 'seq')]
    all_gather x1, waiting for transfers between devices: 82 us -> 16.4 us  [body(): hid = lax.all_gather(near, 'z', axis=0, tiled=True)]
    ppermute x0 -> x14, starting transfers between devices: none -> 43.4 us  [the longest x1 29.6 us: body(): lax.ppermute(got0, 'core', SWAP)]
    pallas_call x0 -> x5, Pallas kernels: none -> 22 us  [call(): pl.pallas_call(kernel, out_shape=[jax.ShapeDtypeStruct(s, d) for s, d in...]
    ppermute x0 -> x14, waiting for transfers between devices: none -> 21 us  [the longest x3 10.7 us: body(): keep = keep + lax.ppermute(v, 'x', shift(NX, d + 1)).astype(F32)]
  transfers between devices with their start and end apart: 3 -> 18, of which waited for: 3 -> 11; matrix products, arithmetic and copies ran while one was open for 2% -> 3% of each run, Pallas kernels for 0% -> 8%
where the time goes in v1:
time: 193 us; the launch traced here: 192 us
  starting transfers between devices  59.6 us (31%)
  waiting for transfers between devices  52 us (27%)
  local copies, waits for them, and re-layouts  22.7 us (12%)
  Pallas kernels  22 us (11%)
  blocking collectives  20.2 us (10%)
  between operations  14.2 us (7%)
    ppermute x1, starting transfers between devices, body(): lax.ppermute(got0, 'core', SWAP)  29.6 us
    pallas_call x5, Pallas kernels, call(): pl.pallas_call(kernel, out_shape=[jax.ShapeDtypeStruct(s, d) for s, d in...  22 us
    all_gather x1, waiting for transfers between devices, body(): hid = lax.all_gather(near, 'z', axis=0, tiled=True)  16.4 us
    unnamed x38, local copies, waits for them, and re-layouts  16.3 us
    ppermute x3, waiting for transfers between devices, body(): keep = keep + lax.ppermute(v, 'x', shift(NX, d + 1)).astype(F32)  10.7 us
    all_to_all x1, blocking collectives, copies(): return lax.all_to_all(flat, axis, 0, 0, tiled=True).reshape((n,) + v.shape)  10.7 us
    all_to_all x1, waiting for transfers between devices, body(): far = lax.all_to_all(wide, ('z', 'x'), 0, 0, tiled=True)  9.68 us
    all_to_all x1, blocking collectives, body(): close = lax.all_to_all(stats, 'y', 0, 0, tiled=True)  9.51 us
  transfers between devices with their start and end apart: 18, of which 11 were waited for; matrix products, arithmetic and copies ran while one was open for 3% of the time, Pallas kernels for 8%

profile of v1, /device:TPU:6, one launch (start us, length us, event | category | flops | bytes accessed | tf_op | source)
XLA Modules:
  0.0 192.3 jit_solution(15335990086506723790)
XLA Ops:
  7.2 1.4 broadcast_in_dim.6
  8.6 4.5 %all-to-all-start = ((bf16[4,16,1024]{2,1,0:T(8,128)(2,1)}), bf16[4,16,1024]{2,1,0:T(8,128)(2,1)S(1)}, u32[]{:S(2)}, u32[]{:S(2)}) async-start(bf16[4,16,1024]{2,1,0:T(8,128)(2,1)} %broadcast_in_dim.6), calls=%async_computation | async-start | bytes 262144 | tf_op jit(solution)/shard_map/all_to_all | solution.py:168
  13.0 3.6 %constant_dynamic-slice_fusion.1 = (bf16[1024,640]{1,0:T(8,128)(2,1)}, bf16[1024,640]{1,0:T(8,128)(2,1)}) fusion(bf16[1024,1280]{1,0:T(8,128)(2,1)} %own.1, s32[]{:T(128)S(6)} %select_n.40, s32[]{:T(128)S(6)} %select_n.38), kind=kLoop, calls=%fused_computation.6 | loop fusion | bytes 5242888 | tf_op jit(solution)/shard_map/dynamic_slice | solution.py:172
  16.7 2.3 %all-to-all-done = bf16[4,16,1024]{2,1,0:T(8,128)(2,1)S(1)} async-done(((bf16[4,16,1024]{2,1,0:T(8,128)(2,1)}), bf16[4,16,1024]{2,1,0:T(8,128)(2,1)S(1)}, u32[]{:S(2)}, u32[]{:S(2)}) %all-to-all-start) | async-done | bytes 131104 | tf_op jit(solution)/shard_map/all_to_all | solution.py:168
  19.1 10.7 %all_to_all.31 = bf16[4,16,4096]{2,1,0:T(8,128)(2,1)} all-to-all(bf16[4,16,4096]{2,1,0:T(8,128)(2,1)S(1)} %broadcast_in_dim.15), channel_id=1, replica_groups=mesh['z'=8,'core'=2,'y'=4,'x'=4] {'x'}, dimensions={0} | all-to-all | bytes 1048576 | tf_op jit(solution)/shard_map/all_to_all | solution.py:168
  29.8 2.0 %collective-permute-start = (bf16[1024,640]{1,0:T(8,128)(2,1)}, bf16[1024,640]{1,0:T(8,128)(2,1)S(1)}, u32[]{:S(2)}, u32[]{:S(2)}) collective-permute-start(bf16[1024,640]{1,0:T(8,128)(2,1)} %get-tuple-element.26), channel_id=1, source_target_pairs={{0,0},{4,4},{8,16},{12,20},{16,8},{20,12},{24,24},{28,28},{1,1},{5... | collective-permute-start | bytes 3932168 | tf_op jit(solution)/shard_map/ppermute | solution.py:178
  31.8 0.6 collective-permute-start.1
  32.3 29.6 %collective-permute-start.2 = (bf16[1024,640]{1,0:T(8,128)(2,1)S(1)}, bf16[1024,640]{1,0:T(8,128)(2,1)S(1)}, u32[]{:S(2)}, u32[]{:S(2)}) collective-permute-start(bf16[1024,640]{1,0:T(8,128)(2,1)S(1)} %collective-permute-done.b0), channel_id=1, source_target_pairs={{0,16},{16,0},{1,17},{17,1},{2,18},{18,2},{3,19},{19,3},{4,20},{20... | collective-permute-start | bytes 3932168 | tf_op jit(solution)/shard_map/ppermute | solution.py:192
  61.9 1.1 copy-done.2
  63.1 0.5 collective-permute-done.1.b1
  63.5 1.8 collective-permute-start.3
  65.3 1.1 copy-done.4
  66.4 1.1 copy-done.6
  68.0 1.0 copy-done.8
  69.8 16.4 %all-gather.2.cloned.1.call-done.hid = bf16[512,4096]{1,0:T(8,128)(2,1)} async-done(((bf16[64,4096]{1,0:T(8,128)(2,1)}), bf16[512,4096]{1,0:T(8,128)(2,1)}) %all-gather.2.cloned.1.call-update) | async-done | bytes 4194320 | tf_op jit(solution)/shard_map/all_gather | solution.py:191
  86.2 2.2 %copy-done.1 = bf16[512,4096]{1,0:T(8,128)(2,1)S(1)} copy-done((bf16[512,4096]{1,0:T(8,128)(2,1)S(1)}, bf16[512,4096]{1,0:T(8,128)(2,1)}, u32[]{:S(2)}) %copy-start.1) | copy-done | bytes 4194328
  88.4 1.3 copy-done.3
  89.7 1.3 copy-done.5
  91.1 1.3 copy-done.7
  92.4 1.3 copy-done.9
  93.7 7.8 %shard_map.67 = (bf16[512,640]{1,0:T(8,128)(2,1)}, f32[4,16,128]{2,1,0:T(8,128)S(1)}, bf16[512,1024]{1,0:T(8,128)(2,1)S(1)}) custom-call(s32[4]{0:T(128)S(1)} %pad_add_fusion.pos, s32[512,1]{1,0:T(8,128)S(1)} %broadcast_in_dim_reshape.9.targets, bf16[1024,640]{1,0:T(8,128)(2,1)S(1)} %copy-done.3, bf16[1024,640]{1,0:T(8,128)(2,1)S(1)} %copy-done.5, ...), custom_call_target="tpu_custom_call" | custom-call | flops 1000 | bytes 1000 | tf_op jit(solution)/shard_map/pallas_call | solution.py:26
  101.6 1.0 copy-done.12
  102.5 9.5 %all_to_all.32.got.near = f32[4,16,128]{2,1,0:T(8,128)S(1)} all-to-all(f32[4,16,128]{2,1,0:T(8,128)S(1)} %get-tuple-element.31), channel_id=1, replica_groups=mesh['z'=8,'core'=2,'y'=4,'x'=4] {'y'}, dimensions={0} | all-to-all | bytes 65536 | tf_op jit(solution)/shard_map/all_to_all | solution.py:209
  112.0 0.6 collective-permute-start.5
  112.6 2.1 %collective-permute-start.6 = (bf16[512,640]{1,0:T(8,128)(2,1)}, bf16[512,640]{1,0:T(8,128)(2,1)}, u32[]{:S(2)}, u32[]{:S(2)}) collective-permute-start(bf16[512,640]{1,0:T(8,128)(2,1)} %get-tuple-element.37.e0), channel_id=1, source_target_pairs={{0,8},{4,12},{8,0},{12,4},{1,9},{5,13},{9,1},{13,5},{2,10},{6,14},... | collective-permute-start | bytes 1966088 | tf_op jit(solution)/shard_map/ppermute | solution.py:211
  114.7 1.1 collective-permute-start.7
  115.8 1.3 shard_map.68
  117.0 7.4 %all-to-all-start.3 = ((f32[32,16,128]{2,1,0:T(8,128)}), f32[32,16,128]{2,1,0:T(8,128)S(1)}, u32[]{:S(2)}, u32[]{:S(2)}) async-start(f32[32,16,128]{2,1,0:T(8,128)} %shard_map.68), calls=%async_computation.3 | async-start | bytes 524288 | tf_op jit(solution)/shard_map/all_to_all | solution.py:214
  124.7 9.7 %all-to-all-done.3.far = f32[32,16,128]{2,1,0:T(8,128)S(1)} async-done(((f32[32,16,128]{2,1,0:T(8,128)}), f32[32,16,128]{2,1,0:T(8,128)S(1)}, u32[]{:S(2)}, u32[]{:S(2)}) %all-to-all-start.3) | async-done | bytes 262176 | tf_op jit(solution)/shard_map/all_to_all | solution.py:214
  134.4 0.6 shard_map.69
  135.0 7.7 %collective-permute-done.5.e1 = bf16[512,640]{1,0:T(8,128)(2,1)} collective-permute-done((bf16[512,640]{1,0:T(8,128)(2,1)}, bf16[512,640]{1,0:T(8,128)(2,1)}, u32[]{:S(2)}, u32[]{:S(2)}) %collective-permute-start.5) | collective-permute-done | bytes 655392 | tf_op jit(solution)/shard_map/ppermute | solution.py:211
  142.7 0.6 collective-permute-done.7.e3
  143.3 7.3 %shard_map.70 = (bf16[512,1280]{1,0:T(8,128)(2,1)S(1)}, bf16[512,1280]{1,0:T(8,128)(2,1)S(1)}, f32[8,16,1024]{2,1,0:T(8,128)S(1)}, bf16[8,16,1024]{2,1,0:T(8,128...) custom-call(s32[4]{0:T(128)S(1)} %pad_add_fusion.pos, ...), custom_call_target="tpu_custom_call" | custom-call | flops 1000 | bytes 1000 | tf_op jit(solution)/shard_map/pallas_call | solution.py:26
  150.7 0.5 collective-permute-start.13
  151.2 1.5 collective-permute-start.10
  152.7 3.2 %collective-permute-start.9 = (bf16[8,16,1024]{2,1,0:T(8,128)(2,1)S(1)}, bf16[8,16,1024]{2,1,0:T(8,128)(2,1)S(1)}, u32[]{:S(2)}, u32[]{:S(2)}) collective-permute-start(bf16[8,16,1024]{2,1,0:T(8,128)(2,1)S(1)} %get-tuple-element.40), channel_id=1, source_target_pairs={{0,1},{1,2},{2,3},{3,0},{4,5},{5,6},{6,7},{7,4},{8,9},{9,10},{10,1... | collective-permute-start | bytes 786440 | tf_op jit(solution)/shard_map/ppermute | solution.py:229
  155.9 6.0 %collective-permute-done.10 = bf16[8,16,1024]{2,1,0:T(8,128)(2,1)S(1)} collective-permute-done((bf16[8,16,1024]{2,1,0:T(8,128)(2,1)S(1)}, bf16[8,16,1024]{2,1,0:T(8,128)(2,1)S(1)}, u32[]{:S(2)}, u32[]{:S(2)}) %collective-permute-start.10) | collective-permute-done | bytes 262176 | tf_op jit(solution)/shard_map/ppermute | solution.py:229
  161.9 4.7 %collective-permute-done.11 = bf16[8,16,1024]{2,1,0:T(8,128)(2,1)S(1)} collective-permute-done((bf16[8,16,1024]{2,1,0:T(8,128)(2,1)S(1)}, bf16[8,16,1024]{2,1,0:T(8,128)(2,1)S(1)}, u32[]{:S(2)}, u32[]{:S(2)}) %collective-permute-start.11) | collective-permute-done | bytes 262176 | tf_op jit(solution)/shard_map/ppermute | solution.py:229
  166.6 0.8 convert_add_fusion
  167.5 1.0 copy-done.15
  168.5 4.3 %all-to-all-start.4 = ((bf16[8,16,1024]{2,1,0:T(8,128)(2,1)}), bf16[8,16,1024]{2,1,0:T(8,128)(2,1)S(1)}, u32[]{:S(2)}, u32[]{:S(2)}) async-start(bf16[8,16,1024]{2,1,0:T(8,128)(2,1)} %convert_add_fusion), calls=%async_computation.4 | async-start | bytes 524288 | tf_op jit(solution)/shard_map/all_to_all | solution.py:234
  173.0 1.0 collective-permute-done.4
  174.1 0.6 reshape.46
  174.8 1.3 copy-done.11
  176.1 1.2 copy-done.16
  177.3 4.9 %shard_map.71 = bf16[1024,1280]{1,0:T(8,128)(2,1)} custom-call(s32[4]{0:T(128)S(1)} %pad_add_fusion.pos, bf16[512,1024]{1,0:T(8,128)(2,1)S(1)} %copy-done.14, bf16[512,1024]{1,0:T(8,128)(2,1)S(1)} %copy-done.16, bf16[512,1280]{1,0:T(8,128)(2,1)S(1)} %copy-done.11, bf16[512,1280]{1,0:T(8,128)(2,1)S(1)} %collective-permute-done.12.g1), custom_call_target="tpu_custom_call" | custom-call | flops 2684354560 | bytes 8388608 | tf_op jit(solution)/shard_map/pallas_call | solution.py:26
  182.3 2.6 %all-to-all-done.4 = bf16[8,16,1024]{2,1,0:T(8,128)(2,1)S(1)} async-done(((bf16[8,16,1024]{2,1,0:T(8,128)(2,1)}), bf16[8,16,1024]{2,1,0:T(8,128)(2,1)S(1)}, u32[]{:S(2)}, u32[]{:S(2)}) %all-to-all-start.4) | async-done | bytes 262176 | tf_op jit(solution)/shard_map/all_to_all | solution.py:234
  184.8 0.7 reduce_sum.12
  (54 shorter events, 1.9 us)
Async XLA Ops:
  8.6 10.4 %all-to-all-start = ((bf16[4,16,1024]{2,1,0:T(8,128)(2,1)}), bf16[4,16,1024]{2,1,0:T(8,128)(2,1)S(1)}, u32[]{:S(2)}, u32[]{:S(2)}) async-start(bf16[4,16,1024]{2,1,0:T(8,128)(2,1)} %broadcast_in_dim.6), calls=%async_computation | async-start | bytes 262144 | tf_op jit(solution)/shard_map/all_to_all | solution.py:168
  13.0 73.2 %all-gather.2.cloned.1.call-start = ((), (), s32[]{:S(2)}) async-start(), calls=%async_computation.5 | async-start | bytes 4718592 | tf_op jit(solution)/shard_map/all_gather | solution.py:191
  13.0 56.0 %copy-start = (bf16[1024,1280]{1,0:T(8,128)(2,1)S(1)}, bf16[1024,1280]{1,0:T(8,128)(2,1)}, u32[]{:S(2)}) copy-start(bf16[1024,1280]{1,0:T(8,128)(2,1)} %own.1) | copy-start | bytes 7864324
  16.7 52.8 %copy-start.17 = (s32[1024]{0:T(1024)S(1)}, s32[1024]{0:T(1024)}, u32[]{:S(2)}) copy-start(s32[1024]{0:T(1024)} %param.6) | copy-start | bytes 12292
  29.8 2.5 %collective-permute-start = (bf16[1024,640]{1,0:T(8,128)(2,1)}, bf16[1024,640]{1,0:T(8,128)(2,1)S(1)}, u32[]{:S(2)}, u32[]{:S(2)}) collective-permute-start(bf16[1024,640]{1,0:T(8,128)(2,1)} %get-tuple-element.26), channel_id=1, source_target_pairs={{0,0},{4,4},{8,16},{12,20},{16,8},{20,12},{24,24},{28,28},{1,1},{5... | collective-permute-start | bytes 3932168 | tf_op jit(solution)/shard_map/ppermute | solution.py:178
  31.8 31.8 %collective-permute-start.1 = (bf16[1024,640]{1,0:T(8,128)(2,1)}, bf16[1024,640]{1,0:T(8,128)(2,1)S(1)}, u32[]{:S(2)}, u32[]{:S(2)}) collective-permute-start(bf16[1024,640]{1,0:T(8,128)(2,1)} %get-tuple-element.27), channel_id=1, source_target_pairs={{0,4},{4,0},{8,20},{12,16},{16,12},{20,8},{24,28},{28,24},{1,5},{5... | collective-permute-start | bytes 3932168 | tf_op jit(solution)/shard_map/ppermute | solution.py:178
  32.3 34.1 %collective-permute-start.2 = (bf16[1024,640]{1,0:T(8,128)(2,1)S(1)}, bf16[1024,640]{1,0:T(8,128)(2,1)S(1)}, u32[]{:S(2)}, u32[]{:S(2)}) collective-permute-start(bf16[1024,640]{1,0:T(8,128)(2,1)S(1)} %collective-permute-done.b0), channel_id=1, source_target_pairs={{0,16},{16,0},{1,17},{17,1},{2,18},{18,2},{3,19},{19,3},{4,20},{20... | collective-permute-start | bytes 3932168 | tf_op jit(solution)/shard_map/ppermute | solution.py:192
  61.9 1.1 copy-start.2
  63.5 4.5 %collective-permute-start.3 = (bf16[1024,640]{1,0:T(8,128)(2,1)S(1)}, bf16[1024,640]{1,0:T(8,128)(2,1)S(1)}, u32[]{:S(2)}, u32[]{:S(2)}) collective-permute-start(bf16[1024,640]{1,0:T(8,128)(2,1)S(1)} %collective-permute-done.1.b1), channel_id=1, source_target_pairs={{0,16},{16,0},{1,17},{17,1},{2,18},{18,2},{3,19},{19,3},{4,20},{20... | collective-permute-start | bytes 3932168 | tf_op jit(solution)/shard_map/ppermute | solution.py:192
  65.3 1.1 copy-start.4
  66.4 1.2 copy-start.6
  68.0 1.1 copy-start.8
  69.1 65.9 %collective-permute-start.8 = (bf16[1024,1280]{1,0:T(8,128)(2,1)S(1)}, bf16[1024,1280]{1,0:T(8,128)(2,1)}, u32[]{:S(2)}, u32[]{:S(2)}) collective-permute-start(bf16[1024,1280]{1,0:T(8,128)(2,1)S(1)} %copy-done), channel_id=1, source_target_pairs={{0,16},{16,0},{1,17},{17,1},{2,18},{18,2},{3,19},{19,3},{4,20},{20... | collective-permute-start | bytes 7864328 | tf_op jit(solution)/shard_map/ppermute | solution.py:194
  86.2 2.2 %copy-start.1 = (bf16[512,4096]{1,0:T(8,128)(2,1)S(1)}, bf16[512,4096]{1,0:T(8,128)(2,1)}, u32[]{:S(2)}) copy-start(bf16[512,4096]{1,0:T(8,128)(2,1)} %all-gather.2.cloned.1.call-done.hid) | copy-start | bytes 12582916
  88.4 1.3 copy-start.3
  89.7 1.3 copy-start.5
  91.1 1.3 copy-start.7
  92.4 1.3 copy-start.9
  93.7 30.8 %copy-start.18 = (f32[1024]{0:T(1024)S(1)}, f32[1024]{0:T(1024)}, u32[]{:S(2)}) copy-start(f32[1024]{0:T(1024)} %param.7) | copy-start | bytes 12292
  101.5 1.0 copy-start.12
  112.0 30.6 %collective-permute-start.5 = (bf16[512,640]{1,0:T(8,128)(2,1)}, bf16[512,640]{1,0:T(8,128)(2,1)}, u32[]{:S(2)}, u32[]{:S(2)}) collective-permute-start(bf16[512,640]{1,0:T(8,128)(2,1)} %get-tuple-element.37.e0), channel_id=1, source_target_pairs={{0,4},{4,8},{8,12},{12,0},{1,5},{5,9},{9,13},{13,1},{2,6},{6,10},{... | collective-permute-start | bytes 1966088 | tf_op jit(solution)/shard_map/ppermute | solution.py:211
  112.6 30.1 %collective-permute-start.6 = (bf16[512,640]{1,0:T(8,128)(2,1)}, bf16[512,640]{1,0:T(8,128)(2,1)}, u32[]{:S(2)}, u32[]{:S(2)}) collective-permute-start(bf16[512,640]{1,0:T(8,128)(2,1)} %get-tuple-element.37.e0), channel_id=1, source_target_pairs={{0,8},{4,12},{8,0},{12,4},{1,9},{5,13},{9,1},{13,5},{2,10},{6,14},... | collective-permute-start | bytes 1966088 | tf_op jit(solution)/shard_map/ppermute | solution.py:211
  114.7 28.6 %collective-permute-start.7 = (bf16[512,640]{1,0:T(8,128)(2,1)}, bf16[512,640]{1,0:T(8,128)(2,1)}, u32[]{:S(2)}, u32[]{:S(2)}) collective-permute-start(bf16[512,640]{1,0:T(8,128)(2,1)} %get-tuple-element.37.e0), channel_id=1, source_target_pairs={{0,12},{4,0},{8,4},{12,8},{1,13},{5,1},{9,5},{13,9},{2,14},{6,2},{... | collective-permute-start | bytes 1966088 | tf_op jit(solution)/shard_map/ppermute | solution.py:211
  117.0 17.3 %all-to-all-start.3 = ((f32[32,16,128]{2,1,0:T(8,128)}), f32[32,16,128]{2,1,0:T(8,128)S(1)}, u32[]{:S(2)}, u32[]{:S(2)}) async-start(f32[32,16,128]{2,1,0:T(8,128)} %shard_map.68), calls=%async_computation.3 | async-start | bytes 524288 | tf_op jit(solution)/shard_map/all_to_all | solution.py:214
  143.3 7.4 %copy-start.13 = (bf16[512,1024]{1,0:T(8,128)(2,1)S(1)}, bf16[512,1024]{1,0:T(8,128)(2,1)}, u32[]{:S(2)}) copy-start(bf16[512,1024]{1,0:T(8,128)(2,1)} %copy-done.12) | copy-start | bytes 3145732
  150.6 16.9 %copy-start.10 = (bf16[512,1280]{1,0:T(8,128)(2,1)}, bf16[512,1280]{1,0:T(8,128)(2,1)S(1)}, u32[]{:S(2)}) copy-start(bf16[512,1280]{1,0:T(8,128)(2,1)S(1)} %get-tuple-element.47.g0) | copy-start | bytes 3932164
  150.6 24.2 %copy-start.14 = (bf16[512,1024]{1,0:T(8,128)(2,1)S(1)}, bf16[512,1024]{1,0:T(8,128)(2,1)}, u32[]{:S(2)}) copy-start(bf16[512,1024]{1,0:T(8,128)(2,1)} %copy-done.12) | copy-start | bytes 3145732
  150.6 17.9 %collective-permute-start.12 = (bf16[512,1280]{1,0:T(8,128)(2,1)S(1)}, bf16[512,1280]{1,0:T(8,128)(2,1)S(1)}, u32[]{:S(2)}, u32[]{:S(2)}) collective-permute-start(bf16[512,1280]{1,0:T(8,128)(2,1)S(1)} %get-tuple-element.43), channel_id=1, source_target_pairs={{0,16},{16,0},{1,17},{17,1},{2,18},{18,2},{3,19},{19,3},{4,20},{20... | collective-permute-start | bytes 3932168 | tf_op jit(solution)/shard_map/ppermute | solution.py:230
  150.7 16.8 %collective-permute-start.13 = (bf16[512,1024]{1,0:T(8,128)(2,1)S(1)}, bf16[512,1024]{1,0:T(8,128)(2,1)S(1)}, u32[]{:S(2)}, u32[]{:S(2)}) collective-permute-start(bf16[512,1024]{1,0:T(8,128)(2,1)S(1)} %copy-done.13), channel_id=1, source_target_pairs={{0,16},{16,0},{1,17},{17,1},{2,18},{18,2},{3,19},{19,3},{4,20},{20... | collective-permute-start | bytes 3145736 | tf_op jit(solution)/shard_map/ppermute | solution.py:218
  151.2 10.7 %collective-permute-start.10 = (bf16[8,16,1024]{2,1,0:T(8,128)(2,1)S(1)}, bf16[8,16,1024]{2,1,0:T(8,128)(2,1)S(1)}, u32[]{:S(2)}, u32[]{:S(2)}) collective-permute-start(bf16[8,16,1024]{2,1,0:T(8,128)(2,1)S(1)} %get-tuple-element.41), channel_id=1, source_target_pairs={{0,2},{1,3},{2,0},{3,1},{4,6},{5,7},{6,4},{7,5},{8,10},{9,11},{10,... | collective-permute-start | bytes 786440 | tf_op jit(solution)/shard_map/ppermute | solution.py:229
  152.7 14.0 %collective-permute-start.11 = (bf16[8,16,1024]{2,1,0:T(8,128)(2,1)S(1)}, bf16[8,16,1024]{2,1,0:T(8,128)(2,1)S(1)}, u32[]{:S(2)}, u32[]{:S(2)}) collective-permute-start(bf16[8,16,1024]{2,1,0:T(8,128)(2,1)S(1)} %get-tuple-element.42), channel_id=1, source_target_pairs={{0,3},{1,0},{2,1},{3,2},{4,7},{5,4},{6,5},{7,6},{8,11},{9,8},{10,9... | collective-permute-start | bytes 786440 | tf_op jit(solution)/shard_map/ppermute | solution.py:229
  152.7 14.0 %collective-permute-start.9 = (bf16[8,16,1024]{2,1,0:T(8,128)(2,1)S(1)}, bf16[8,16,1024]{2,1,0:T(8,128)(2,1)S(1)}, u32[]{:S(2)}, u32[]{:S(2)}) collective-permute-start(bf16[8,16,1024]{2,1,0:T(8,128)(2,1)S(1)} %get-tuple-element.40), channel_id=1, source_target_pairs={{0,1},{1,2},{2,3},{3,0},{4,5},{5,6},{6,7},{7,4},{8,9},{9,10},{10,1... | collective-permute-start | bytes 786440 | tf_op jit(solution)/shard_map/ppermute | solution.py:229
  167.5 1.0 copy-start.15
  168.5 16.4 %all-to-all-start.4 = ((bf16[8,16,1024]{2,1,0:T(8,128)(2,1)}), bf16[8,16,1024]{2,1,0:T(8,128)(2,1)S(1)}, u32[]{:S(2)}, u32[]{:S(2)}) async-start(bf16[8,16,1024]{2,1,0:T(8,128)(2,1)} %convert_add_fusion), calls=%async_computation.4 | async-start | bytes 524288 | tf_op jit(solution)/shard_map/all_to_all | solution.py:234
  172.8 1.2 collective-permute-start.4
  174.8 1.3 copy-start.11
  176.1 1.2 copy-start.16
Sparse Core Ops, SparseCore 0:
  29.9 56.2 all-gather.1

commit v2 on v1

--- a/solution.py
+++ b/solution.py
@@ -1,3 +1,5 @@
+import functools
+
 import jax
 import jax.numpy as jnp
 from jax import lax
@@ -22,7 +24,7 @@
 ANY = pl.BlockSpec(memory_space=pl.ANY)
 
 
-def call(kernel, outs, args, scratch=(), flops=1000, moved=1000, far=0):
+def call(kernel, outs, args, scratch=(), flops=1000, moved=1000, far=0, vmem=24):
     return pl.pallas_call(
         kernel,
         out_shape=[jax.ShapeDtypeStruct(s, d) for s, d in outs],
@@ -30,46 +32,97 @@
         out_specs=[VMEM] * len(outs),
         scratch_shapes=list(scratch),
         cost_estimate=pl.CostEstimate(flops=flops, bytes_accessed=moved, transcendentals=0),
-        compiler_params=pltpu.CompilerParams(vmem_limit_bytes=24 * 2**20),
+        compiler_params=pltpu.CompilerParams(vmem_limit_bytes=vmem * 2**20),
     )(*args)
 
 
-def logits_kernel(pos, targets, b0, b1, b2, b3, hid, *refs):
-    e_out, stats_out, slice_out, acc, hid_v, sems = refs
+def early_kernel(count, pos, targets, *refs):
+    pieces, blocks = refs[:count], refs[count : count + 4]
+    e_out, table_out, slice_out, acc, hid_v, block_v, hid_sem, block_sem = refs[count + 4 :]
     z, c, y, x = (pos[i] for i in range(4))
-    width, group = b0.shape
-    rows = e_out.shape[0]
+    _, width, group = block_v.shape
+    per_z = pieces[0].shape[0]
+    block_copies = [
+        pltpu.make_async_copy(b, block_v.at[i], block_sem.at[i]) for i, b in enumerate(blocks)
+    ]
     copies = []
+    for i, p in enumerate(pieces):
+        first = lax.rem(z + i + 3 * (i > 2), NZ) * per_z
+        at = pl.ds(pl.multiple_of(first, 64), per_z)
+        copies.append(pltpu.make_async_copy(p, hid_v.at[at], hid_sem.at[i]))
+    for copy in copies + block_copies:
+        copy.start()
+    for ahead in (3, 4, 5):
+        hid_v[pl.ds(pl.multiple_of(lax.rem(z + ahead, NZ) * per_z, 64), per_z)] = jnp.zeros(
+            (per_z, hid_v.shape[1]), BF16
+        )
+    for copy in copies:
+        copy.wait()
+    multiply(hid_v, block_v, block_copies, acc, c, y)
+    slice_out[...] = columns(hid_v, y, width)
+    e_out[...], table_out[...] = soften(acc[...], targets[...], z, y, x)
+
+
+def late_kernel(pos, targets, e_in, table_in, slice_in, p3, p5, p4a, p4b, b0, b1, b2, b3, *refs):
+    e_out, slice_out, stats_out, table, acc, hid_v, block_v, hid_sem, block_sem = refs
+    z, c, y, x = (pos[i] for i in range(4))
+    _, width, group = block_v.shape
+    per_z = p3.shape[0]
+    block_copies = [
+        pltpu.make_async_copy(b, block_v.at[i], block_sem.at[i])
+        for i, b in enumerate((b0, b1, b2, b3))
+    ]
+    copies = [
+        pltpu.make_async_copy(p, hid_v.at[pl.ds(first, p.shape[0])], hid_sem.at[i])
+        for i, (p, first) in enumerate(
+            ((p3, 0), (p4a, per_z), (p4b, per_z + per_z // 2), (p5, 2 * per_z))
+        )
+    ]
+    for copy in copies + block_copies:
+        copy.start()
+    e_out[...] = e_in[...]
+    slice_out[...] = slice_in[...]
+    table[...] = table_in[...]
+    for copy in copies:
+        copy.wait()
+    multiply(hid_v, block_v, block_copies, acc, c, y)
+    mine = columns(hid_v, y, width)
+    for i in range(3):
+        part = slice(i * per_z, (i + 1) * per_z)
+        here = pl.ds(pl.multiple_of(lax.rem(z + 3 + i, NZ) * per_z, 64), per_z)
+        slice_out[here] = mine[part]
+        e_out[here], table[here] = soften(acc[part], targets[here], z, y, x)
+    flat = table[...].T
+    packed = pack([flat[0:1], flat[1:2], flat[2:3]])
+    for i in range(stats_out.shape[0]):
+        stats_out[i] = packed
+
+
+def columns(hid_v, origin, width):
+    return hid_v[:, pl.ds(pl.multiple_of(origin * width, 128), width)]
+
+
+def multiply(hid_v, block_v, block_copies, acc, c, y):
+    width = block_v.shape[1]
     for i in range(4):
         core = c if i < 2 else 1 - c
-        origin = 2 * core + lax.rem(y + i, 2)
-        cols = pl.ds(pl.multiple_of(origin * width, 128), width)
-        copies.append(pltpu.make_async_copy(hid.at[:, cols], hid_v.at[i], sems.at[i]))
-    for copy in copies:
-        copy.start()
-    for i, block in enumerate((b0, b1, b2, b3)):
-        copies[i].wait()
-        term = jnp.dot(hid_v[i], block[...], preferred_element_type=F32)
+        block_copies[i].wait()
+        mine = columns(hid_v, 2 * core + lax.rem(y + i, 2), width)
+        term = jnp.dot(mine, block_v[i], preferred_element_type=F32)
         acc[...] = term if i == 0 else acc[...] + term
 
-        @pl.when((c if i < 2 else 1 - c) * 2 + lax.rem(y + i, 2) == y)
-        def _():
-            slice_out[...] = hid_v[i]
-
-    logits = acc[...]
+
+def soften(logits, targets, z, y, x):
+    rows, group = logits.shape
     top = jnp.max(logits, axis=1, keepdims=True)
     e = jnp.exp(logits - top)
     total = jnp.sum(e, axis=1, keepdims=True)
     first = ((z * NC + y // 2) * NX + x) * (2 * group) + lax.rem(y, 2) * group
     ids = first + lax.broadcasted_iota(jnp.int32, (rows, group), 1)
-    picked = jnp.sum(jnp.where(ids == targets[...], logits, 0.0), axis=1, keepdims=True)
-    e_out[...] = e.astype(BF16)
+    picked = jnp.sum(jnp.where(ids == targets, logits, 0.0), axis=1, keepdims=True)
     lane = lax.broadcasted_iota(jnp.int32, (rows, 128), 1)
     table = jnp.where(lane == 0, top, jnp.where(lane == 1, total, jnp.where(lane == 2, picked, 0.0)))
-    flat = table.T
-    packed = pack([flat[0:1], flat[1:2], flat[2:3]])
-    for i in range(stats_out.shape[0]):
-        stats_out[i] = packed
+    return e.astype(BF16), table
 
 
 def pack(vectors):
@@ -87,39 +140,36 @@
     return top, jnp.sum(s * jnp.exp(m - top[None]), axis=0), jnp.sum(p, axis=0)
 
 
-def near_kernel(pos, got, out):
+def wide_kernel(pos, got, out):
+    z, x = pos[0], pos[3]
     m, s, p = merged(got[...])
-    packed = jnp.concatenate([m, s, p, jnp.zeros_like(m)], axis=0)
-    for i in range(out.shape[0]):
-        out[i] = packed
-
-
-def far_kernel(pos, far, near, weights, vec_out, log_prob_out):
-    y = pos[2]
-    m, s, p = (unpack(v) for v in merged(far[...]))
+    out[...] = jnp.concatenate([m, s, p, got[z * NX + x][0:4]], axis=0)
+
+
+def total_kernel(pos, t0, t1, t2, t3, weights, vec_out, log_prob_out):
+    tables = [t[...] for t in (t0, t1, t2, t3)]
+    m, s, p = (unpack(v) for v in merged(jnp.stack(tables)))
     log_total = m + jnp.log(s)
     log_prob = p - log_total
     w = weights[...]
-    rows = []
-    for d in range(NY):
-        local = unpack(near[lax.rem(y + NY - d, NY)][0:4])
-        rows.append(-w * jnp.exp(local - log_total))
+    rows = [-w * jnp.exp(unpack(t[12:16]) - log_total) for t in tables]
     rows.append(w * (1.0 - jnp.exp(log_prob)))
     rows.append(jnp.zeros((3, m.shape[1]), F32))
     vec_out[...] = jnp.concatenate(rows, axis=0)
     log_prob_out[...] = jnp.broadcast_to(log_prob, log_prob_out.shape)
 
 
-def grad_kernel(pos, targets, vec, e0, e1, e2, e3, own, other, g0, g1, keep, s1, s2, s3, part):
+def grad_kernel(pos, targets, vec, e0, e1, e2, e2b, e3, own, other, g0, g1, keep, s1, s2, s3, part):
     z, c, y, x = (pos[i] for i in range(4))
     rows, group = e0.shape
     cols = jnp.concatenate([vec[...], jnp.zeros((120, rows), F32)], axis=0).T
     t = targets[...]
-    for d, e in enumerate((e0, e1, e2, e3)):
+    opposite = jnp.concatenate([e2[...], e2b[...]], axis=0)
+    for d, e in enumerate((e0[...], e1[...], opposite, e3[...])):
         g = lax.rem(y + NY - d, NY)
         first = ((z * NC + g // 2) * NX + x) * (2 * group) + lax.rem(g, 2) * group
         ids = first + lax.broadcasted_iota(jnp.int32, (rows, group), 1)
-        value = jnp.where(ids == t, cols[:, 4:5], e[...].astype(F32) * cols[:, d : d + 1])
+        value = jnp.where(ids == t, cols[:, 4:5], e.astype(F32) * cols[:, d : d + 1])
         value = value.astype(BF16)
         at = pl.ds(pl.multiple_of(lax.rem(g, 2) * group, 128), group)
         same = g // 2 == c
@@ -168,6 +218,7 @@
         return lax.all_to_all(flat, axis, 0, 0, tiled=True).reshape((n,) + v.shape)
 
     near = copies(hidden, NY, "y")
+
     def block(k):
         return lax.dynamic_slice_in_dim(head, ((y + k) % 2) * group, group, 1)
 
@@ -188,34 +239,63 @@
 
     my_targets, my_weights = ordered(targets)[:, None], ordered(weights)[None]
 
-    hid = lax.all_gather(near, "z", axis=0, tiled=True)
-    twin0, twin1 = lax.ppermute(got0, "core", SWAP), lax.ppermute(got1, "core", SWAP)
-    twin0, twin1, head_later = tie(twin0, twin1, head)
-    other = lax.ppermute(head_later, "core", SWAP)
-
     size = NZ * per_z
-    e, stats, mine = call(
-        logits_kernel,
-        [((size, group), BF16), ((NY, 16, 128), F32), ((size, width), BF16)],
-        (pos, my_targets, got0, got1, twin0, twin1, hid),
-        scratch=[
-            pltpu.VMEM((size, group), F32),
-            pltpu.VMEM((NY, size, width), BF16),
+    def scratch(rows, pieces):
+        return [
+            pltpu.VMEM((rows, group), F32),
+            pltpu.VMEM((rows, NY * width), BF16),
+            pltpu.VMEM((NY, width, group), BF16),
+            pltpu.SemaphoreType.DMA((pieces,)),
             pltpu.SemaphoreType.DMA((NY,)),
-        ],
-        far=1,
+        ]
+
+    pieces, flying = {0: near}, {1: near, -1: near}
+    for step in range(1, 5):
+        if step == 3:
+            got0, got1, head_later, pos, my_targets, my_weights, *tied = tie(
+                got0, got1, head, pos, my_targets, my_weights, flying[1], flying[-1]
+            )
+            flying = {1: tied[0], -1: tied[1]}
+            twin0, twin1 = lax.ppermute(got0, "core", SWAP), lax.ppermute(got1, "core", SWAP)
+            other = lax.ppermute(head_later, "core", SWAP)
+        if step == 4:
+            blocks = (got0, got1, twin0, twin1)
+            hid = [pieces[r] for r in (0, 1, 2, 6, 7)]
+            e, table, mine = call(
+                functools.partial(early_kernel, len(hid)),
+                [((size, group), BF16), ((size, 128), F32), ((size, width), BF16)],
+                (pos, my_targets, *hid, *blocks),
+                scratch=scratch(size, len(hid)),
+                far=len(hid) + 4,
+                vmem=60,
+                flops=2 * size * NY * width * group,
+                moved=10 * 2**20,
+            )
+            e, table, mine, *tied = tie(e, table, mine, flying[1], flying[-1])
+            flying = {1: tied[0], -1: tied[1]}
+            flying = {1: flying[1][: per_z // 2], -1: flying[-1][per_z // 2 :]}
+        for d in (1, -1):
+            flying[d] = lax.ppermute(flying[d], "z", shift(NZ, d))
+            pieces[-d * step if step == 4 else (-d * step) % NZ] = flying[d]
+
+    e, mine, stats = call(
+        late_kernel,
+        [((size, group), BF16), ((size, width), BF16), ((NZ * NX, 16, 128), F32)],
+        (pos, my_targets, e, table, mine, *[pieces[r] for r in (3, 5, -4, 4)], *blocks),
+        scratch=[pltpu.VMEM((size, 128), F32)] + scratch(3 * per_z, 4),
+        far=8,
+        vmem=56,
     )
 
-    close = lax.all_to_all(stats, "y", 0, 0, tiled=True)
-    close, e, mine = tie(close, e, mine)
-    exps = [e] + [lax.ppermute(e, "y", shift(NY, d)) for d in (2, 1, 3)]
-    exps = [exps[0], exps[2], exps[1], exps[3]]
-    (wide,) = call(near_kernel, [((NZ * NX, 16, 128), F32)], (pos, close))
-    far = lax.all_to_all(wide, ("z", "x"), 0, 0, tiled=True)
-    vec, lp = call(
-        far_kernel, [((8, size), F32), ((8, size), F32)], (pos, far, close, my_weights)
-    )
+    e1, e3 = lax.ppermute(e, "y", shift(NY, 1)), lax.ppermute(e, "y", shift(NY, -1))
+    far = lax.all_to_all(stats, ("z", "x"), 0, 0, tiled=True)
+    e2 = lax.ppermute(e1[: size // 2], "y", shift(NY, 1))
+    e2b = lax.ppermute(e3[size // 2 :], "y", shift(NY, -1))
+    (wide,) = call(wide_kernel, [((16, 128), F32)], (pos, far))
+    tables = [wide] + [lax.ppermute(wide, "y", shift(NY, d)) for d in (1, 2, 3)]
+    vec, lp = call(total_kernel, [((8, size), F32), ((8, size), F32)], (pos, *tables, my_weights))
     twin_mine = lax.ppermute(mine, "core", SWAP)
+    exps = (e, e1, e2, e2b, e3)
 
     kept, sent, keep, *send = call(
         grad_kernel,
@@ -225,13 +305,8 @@
         (pos, my_targets, vec, *exps, head, other),
         scratch=[pltpu.VMEM((NZ, NX, rows, width), F32)],
     )
-    for d, v in enumerate(send):
-        keep = keep + lax.ppermute(v, "x", shift(NX, d + 1)).astype(F32)
+    terms = [lax.ppermute(v, "x", shift(NX, d + 1)) for d, v in enumerate(send)]
     twin_kept = lax.ppermute(sent, "core", SWAP)
-    keep, twin_kept, twin_mine = tie(keep, twin_kept, twin_mine)
-
-    total = keep.astype(BF16).reshape(NZ * rows, width)
-    got = lax.all_to_all(total, "z", 0, 0, tiled=True)
     (head_grad,) = call(
         head_kernel,
         [((width, columns), BF16)],
@@ -239,6 +314,12 @@
         flops=2 * NZ * NC * per_z * columns * width,
         moved=8 * 2**20,
     )
+    head_grad, *terms = tie(head_grad, *terms)
+
+    for term in terms:
+        keep = keep + term.astype(F32)
+    total = keep.astype(BF16).reshape(NZ * rows, width)
+    got = lax.all_to_all(total, "z", 0, 0, tiled=True)
     hidden_grad = jnp.sum(got.reshape(NZ, rows, width).astype(F32), axis=0).astype(BF16)
 
     log_prob = lp[0]

time: 193 us -> 175 us (0.907)
  blocking collectives: 20.2 us -> 0 us
  between operations: 14.2 us -> 0.87 us
  Pallas kernels: 22 us -> 31.2 us
  waiting for transfers between devices: 52 us -> 61 us
  local copies, waits for them, and re-layouts: 22.7 us -> 13.9 us
  starting transfers between devices: 59.6 us -> 64.4 us
    ppermute x1, starting transfers between devices: 29.6 us -> 0.01 us  [body(): lax.ppermute(got0, 'core', SWAP)]
    ppermute x6 -> x18, waiting for transfers between devices: 19 us -> 45 us  [the longest x8 25.1 us: body(): flying[d] = lax.ppermute(flying[d], 'z', shift(NZ, d))]
    all_to_all x2 -> x0, blocking collectives: 20.2 us -> none  [the longest x1 10.7 us: copies(): return lax.all_to_all(flat, axis, 0, 0, tiled=True).reshape((n,) + v.shape)]
    ppermute x6 -> x18, starting transfers between devices: 8.42 us -> 27.9 us  [the longest x8 16.9 us: body(): flying[d] = lax.ppermute(flying[d], 'z', shift(NZ, d))]
    all_gather x1 -> x0, waiting for transfers between devices: 16.4 us -> none  [body(): hid = lax.all_gather(near, 'z', axis=0, tiled=True)]
    unnamed x38 -> x24, local copies, waits for them, and re-layouts: 16.3 us -> 1.84 us
    all_to_all x1, waiting for transfers between devices: 9.68 us -> 0.01 us  [body(): far = lax.all_to_all(stats, ('z', 'x'), 0, 0, tiled=True)]
    ppermute x2, starting transfers between devices: 2.54 us -> 11.8 us  [hand_over(): return lax.ppermute(v, ('core', 'y'), perm)]
  transfers between devices with their start and end apart: 18 -> 30, of which waited for: 11 -> 15; matrix products, arithmetic and copies ran while one was open for 3% -> 6% of each run, Pallas kernels for 8% -> 14%
where the time goes in v2:
time: 175 us; the launch traced here: 174 us
  starting transfers between devices  64.4 us (37%)
  waiting for transfers between devices  61 us (35%)
  Pallas kernels  31.2 us (18%)
  local copies, waits for them, and re-layouts  13.9 us (8%)
  other arithmetic  2.11 us (1%)
    pallas_call x6, Pallas kernels, call(): pl.pallas_call(kernel, out_shape=[jax.ShapeDtypeStruct(s, d) for s, d in...  31.2 us
    ppermute x8, waiting for transfers between devices, body(): flying[d] = lax.ppermute(flying[d], 'z', shift(NZ, d))  25.1 us
    ppermute x8, starting transfers between devices, body(): flying[d] = lax.ppermute(flying[d], 'z', shift(NZ, d))  16.9 us
    ppermute x2, starting transfers between devices, hand_over(): return lax.ppermute(v, ('core', 'y'), perm)  11.8 us
    all_to_all x1, starting transfers between devices, body(): far = lax.all_to_all(stats, ('z', 'x'), 0, 0, tiled=True)  9.52 us
    all_to_all x1, waiting for transfers between devices, body(): got = lax.all_to_all(total, 'z', 0, 0, tiled=True)  9.38 us
    all_to_all x2, starting transfers between devices, copies(): return lax.all_to_all(flat, axis, 0, 0, tiled=True).reshape((n,) + v.shape)  9.23 us
    ppermute x3, waiting for transfers between devices, body(): terms = [lax.ppermute(v, 'x', shift(NX, d + 1)) for d, v in enumerate(send)]  8.06 us
  transfers between devices with their start and end apart: 30, of which 15 were waited for; matrix products, arithmetic and copies ran while one was open for 6% of the time, Pallas kernels for 14%

profile of v2, /device:TPU:6, one launch (start us, length us, event | category | flops | bytes accessed | tf_op | source)
XLA Modules:
  0.0 173.5 jit_solution(15917174522164672526)
XLA Ops:
  0.6 1.4 broadcast_in_dim.6
  2.1 4.5 %all-to-all-start = ((bf16[4,16,1024]{2,1,0:T(8,128)(2,1)}), bf16[4,16,1024]{2,1,0:T(8,128)(2,1)S(1)}, u32[]{:S(2)}, u32[]{:S(2)}) async-start(bf16[4,16,1024]{2,1,0:T(8,128)(2,1)} %broadcast_in_dim.6), calls=%async_computation | async-start | bytes 262144 | tf_op jit(solution)/shard_map/all_to_all | solution.py:218
  6.5 3.6 %constant_dynamic-slice_fusion.1 = (bf16[1024,640]{1,0:T(8,128)(2,1)}, bf16[1024,640]{1,0:T(8,128)(2,1)}) fusion(bf16[1024,1280]{1,0:T(8,128)(2,1)} %own.1, s32[]{:T(128)S(6)} %select_n.39, s32[]{:T(128)S(6)} %select_n.37), kind=kLoop, calls=%fused_computation.6 | loop fusion | bytes 5242888 | tf_op jit(solution)/shard_map/dynamic_slice | solution.py:223
  10.1 2.4 %all-to-all-done = bf16[4,16,1024]{2,1,0:T(8,128)(2,1)S(1)} async-done(((bf16[4,16,1024]{2,1,0:T(8,128)(2,1)}), bf16[4,16,1024]{2,1,0:T(8,128)(2,1)S(1)}, u32[]{:S(2)}, u32[]{:S(2)}) %all-to-all-start) | async-done | bytes 131104 | tf_op jit(solution)/shard_map/all_to_all | solution.py:218
  12.5 0.8 broadcast_in_dim.15
  13.3 4.8 %all-to-all-start.1 = ((bf16[4,16,4096]{2,1,0:T(8,128)(2,1)}), bf16[4,16,4096]{2,1,0:T(8,128)(2,1)S(1)}, u32[]{:S(2)}, u32[]{:S(2)}) async-start(bf16[4,16,4096]{2,1,0:T(8,128)(2,1)} %broadcast_in_dim.15), calls=%async_computation.1 | async-start | bytes 1048576 | tf_op jit(solution)/shard_map/all_to_all | solution.py:218
  18.1 11.3 %collective-permute-start = (bf16[1024,640]{1,0:T(8,128)(2,1)}, bf16[1024,640]{1,0:T(8,128)(2,1)}, u32[]{:S(2)}, u32[]{:S(2)}) collective-permute-start(bf16[1024,640]{1,0:T(8,128)(2,1)} %get-tuple-element.37), channel_id=1, source_target_pairs={{0,0},{4,4},{8,16},{12,20},{16,8},{20,12},{24,24},{28,28},{1,1},{5... | collective-permute-start | bytes 3932168 | tf_op jit(solution)/shard_map/ppermute | solution.py:229
  30.0 1.9 %collective-permute-start.2 = (bf16[64,4096]{1,0:T(8,128)(2,1)S(1)}, bf16[64,4096]{1,0:T(8,128)(2,1)}, u32[]{:S(2)}, u32[]{:S(2)}) collective-permute-start(bf16[64,4096]{1,0:T(8,128)(2,1)S(1)} %bitcast.13), channel_id=1, source_target_pairs={{0,32},{32,64},{64,96},{96,128},{128,160},{160,192},{192,224},{224... | collective-permute-start | bytes 1572872 | tf_op jit(solution)/shard_map/ppermute | solution.py:278
  31.9 4.0 %collective-permute-start.4 = (bf16[64,4096]{1,0:T(8,128)(2,1)S(1)}, bf16[64,4096]{1,0:T(8,128)(2,1)}, u32[]{:S(2)}, u32[]{:S(2)}) collective-permute-start(bf16[64,4096]{1,0:T(8,128)(2,1)S(1)} %bitcast.14), channel_id=1, source_target_pairs={{0,224},{32,0},{64,32},{96,64},{128,96},{160,128},{192,160},{224,1... | collective-permute-start | bytes 1572872 | tf_op jit(solution)/shard_map/ppermute | solution.py:278
  35.9 12.5 %collective-permute-done.2.refs_4_ = bf16[64,4096]{1,0:T(8,128)(2,1)} collective-permute-done((bf16[64,4096]{1,0:T(8,128)(2,1)S(1)}, bf16[64,4096]{1,0:T(8,128)(2,1)}, u32[]{:S(2)}, u32[]{:S(2)}) %collective-permute-start.2) | collective-permute-done | bytes 524320 | tf_op jit(solution)/shard_map/ppermute | solution.py:278
  48.4 3.5 %collective-permute-start.5 = (bf16[64,4096]{1,0:T(8,128)(2,1)}, bf16[64,4096]{1,0:T(8,128)(2,1)}, u32[]{:S(2)}, u32[]{:S(2)}) collective-permute-start(bf16[64,4096]{1,0:T(8,128)(2,1)} %collective-permute-done.4.refs_1_), channel_id=1, source_target_pairs={{0,224},{32,0},{64,32},{96,64},{128,96},{160,128},{192,160},{224,1... | collective-permute-start | bytes 1572872 | tf_op jit(solution)/shard_map/ppermute | solution.py:278
  52.9 6.2 %collective-permute-done.3.refs_3_ = bf16[64,4096]{1,0:T(8,128)(2,1)} collective-permute-done((bf16[64,4096]{1,0:T(8,128)(2,1)}, bf16[64,4096]{1,0:T(8,128)(2,1)}, u32[]{:S(2)}, u32[]{:S(2)}) %collective-permute-start.3) | collective-permute-done | bytes 524320 | tf_op jit(solution)/shard_map/ppermute | solution.py:278
  59.6 3.6 %collective-permute-start.9 = (bf16[64,4096]{1,0:T(8,128)(2,1)}, bf16[64,4096]{1,0:T(8,128)(2,1)}, u32[]{:S(2)}, u32[]{:S(2)}) collective-permute-start(bf16[64,4096]{1,0:T(8,128)(2,1)} %collective-permute-done.5.refs_2_), channel_id=1, source_target_pairs={{0,224},{32,0},{64,32},{96,64},{128,96},{160,128},{192,160},{224,1... | collective-permute-start | bytes 1572872 | tf_op jit(solution)/shard_map/ppermute | solution.py:278
  63.2 0.9 copy.17.targets
  64.1 2.2 %collective-permute-done.7.refs_8_.b3 = bf16[1024,640]{1,0:T(8,128)(2,1)} collective-permute-done((bf16[1024,640]{1,0:T(8,128)(2,1)}, bf16[1024,640]{1,0:T(8,128)(2,1)}, u32[]{:S(2)}, u32[]{:S(2)}) %collective-permute-start.7) | collective-permute-done | bytes 1310752 | tf_op jit(solution)/shard_map/ppermute | solution.py:259
  66.2 10.2 %shard_map.67 = (bf16[512,640]{1,0:T(8,128)(2,1)}, f32[512,128]{1,0:T(8,128)}, bf16[512,1024]{1,0:T(8,128)(2,1)}) custom-call(s32[4]{0:T(128)} %pad_add_fusion.pos, s32[512,1]{1,0:T(8,128)} %copy.17.targets, bf16[64,4096]{1,0:T(8,128)(2,1)} %bitcast.15, bf16[64,4096]{1,0:T(8,128)(2,1)} %collective-permute-done.4.refs_1_, ...), custom_call_target="tpu_custom_call" | custom-call | flops 2684354560 | bytes 10485760 | tf_op jit(solution)/shard_map/pallas_call | solution.py:28
  76.5 2.4 %collective-permute-start.10 = (bf16[32,4096]{1,0:T(8,128)(2,1)S(1)}, bf16[32,4096]{1,0:T(8,128)(2,1)S(1)}, u32[]{:S(2)}, u32[]{:S(2)}) collective-permute-start(bf16[32,4096]{1,0:T(8,128)(2,1)S(1)} %slice.15), channel_id=1, source_target_pairs={{0,32},{32,64},{64,96},{96,128},{128,160},{160,192},{192,224},{224... | collective-permute-start | bytes 786440 | tf_op jit(solution)/shard_map/ppermute | solution.py:278
  79.0 1.0 slice.16
  80.0 1.4 collective-permute-start.11
  81.4 5.5 %collective-permute-done.10.p4a = bf16[32,4096]{1,0:T(8,128)(2,1)S(1)} collective-permute-done((bf16[32,4096]{1,0:T(8,128)(2,1)S(1)}, bf16[32,4096]{1,0:T(8,128)(2,1)S(1)}, u32[]{:S(2)}, u32[]{:S(2)}) %collective-permute-start.10) | collective-permute-done | bytes 262176 | tf_op jit(solution)/shard_map/ppermute | solution.py:278
  86.9 0.8 collective-permute-done.11.p4b
  87.7 0.7 copy-done.9
  88.4 7.6 %shard_map.68 = (bf16[512,640]{1,0:T(8,128)(2,1)}, bf16[512,1024]{1,0:T(8,128)(2,1)}, f32[32,16,128]{2,1,0:T(8,128)}) custom-call(s32[4]{0:T(128)} %pad_add_fusion.pos, s32[512,1]{1,0:T(8,128)} %copy.17.targets, bf16[512,640]{1,0:T(8,128)(2,1)} %get-tuple-element.49.e_in, f32[512,128]{1,0:T(8,128)} %get-tuple-element.50.table_in, ...), custom_call_target="tpu_custom_call" | custom-call | flops 1000 | bytes 1000 | tf_op jit(solution)/shard_map/pallas_call | solution.py:28
  96.0 1.3 collective-permute-start.16
  97.3 2.0 %collective-permute-start.18 = (bf16[512,640]{1,0:T(8,128)(2,1)}, bf16[512,640]{1,0:T(8,128)(2,1)}, u32[]{:S(2)}, u32[]{:S(2)}) collective-permute-start(bf16[512,640]{1,0:T(8,128)(2,1)} %get-tuple-element.58.e0), channel_id=1, source_target_pairs={{0,12},{4,0},{8,4},{12,8},{1,13},{5,1},{9,5},{13,9},{2,14},{6,2},{... | collective-permute-start | bytes 1966088 | tf_op jit(solution)/shard_map/ppermute | solution.py:290
  99.3 9.5 %all-to-all-start.2 = ((f32[32,16,128]{2,1,0:T(8,128)}), f32[32,16,128]{2,1,0:T(8,128)}, u32[]{:S(2)}, u32[]{:S(2)}) async-start(f32[32,16,128]{2,1,0:T(8,128)} %get-tuple-element.54), calls=%async_computation.2 | async-start | bytes 524288 | tf_op jit(solution)/shard_map/all_to_all | solution.py:291
  108.8 4.8 %collective-permute-done.16.e1 = bf16[512,640]{1,0:T(8,128)(2,1)S(1)} collective-permute-done((bf16[512,640]{1,0:T(8,128)(2,1)}, bf16[512,640]{1,0:T(8,128)(2,1)S(1)}, u32[]{:S(2)}, u32[]{:S(2)}) %collective-permute-start.16) | collective-permute-done | bytes 655392 | tf_op jit(solution)/shard_map/ppermute | solution.py:290
  113.7 0.8 slice.20
  114.5 1.7 slice.21
  116.2 3.1 %collective-permute-start.19 = (bf16[256,640]{1,0:T(8,128)(2,1)}, bf16[256,640]{1,0:T(8,128)(2,1)}, u32[]{:S(2)}, u32[]{:S(2)}) collective-permute-start(bf16[256,640]{1,0:T(8,128)(2,1)} %slice.21), channel_id=1, source_target_pairs={{0,12},{4,0},{8,4},{12,8},{1,13},{5,1},{9,5},{13,9},{2,14},{6,2},{... | collective-permute-start | bytes 983048 | tf_op jit(solution)/shard_map/ppermute | solution.py:293
  119.4 1.0 shard_map.69.t0
  120.5 1.5 collective-permute-start.13
  122.0 3.4 %collective-permute-done.12.t1 = f32[16,128]{1,0:T(8,128)S(1)} collective-permute-done((f32[16,128]{1,0:T(8,128)S(1)}, f32[16,128]{1,0:T(8,128)S(1)}, u32[]{:S(2)}, u32[]{:S(2)}) %collective-permute-start.12) | collective-permute-done | bytes 8224 | tf_op jit(solution)/shard_map/ppermute | solution.py:295
  125.7 3.3 %collective-permute-done.14.t3 = f32[16,128]{1,0:T(8,128)S(1)} collective-permute-done((f32[16,128]{1,0:T(8,128)S(1)}, f32[16,128]{1,0:T(8,128)S(1)}, u32[]{:S(2)}, u32[]{:S(2)}) %collective-permute-start.14) | collective-permute-done | bytes 8224 | tf_op jit(solution)/shard_map/ppermute | solution.py:295
  129.7 1.1 copy-done.2
  130.7 6.8 %shard_map.71 = (bf16[512,1280]{1,0:T(8,128)(2,1)S(1)}, bf16[512,1280]{1,0:T(8,128)(2,1)S(1)}, f32[8,16,1024]{2,1,0:T(8,128)S(1)}, bf16[8,16,1024]{2,1,0:T(8,128...) custom-call(s32[4]{0:T(128)S(1)} %copy-done.3, s32[512,1]{1,0:T(8,128)S(1)} %copy-done.1, ...), custom_call_target="tpu_custom_call" | custom-call | flops 1000 | bytes 1000 | tf_op jit(solution)/shard_map/pallas_call | solution.py:28
  138.4 1.9 %collective-permute-start.23 = (bf16[8,16,1024]{2,1,0:T(8,128)(2,1)S(1)}, bf16[8,16,1024]{2,1,0:T(8,128)(2,1)S(1)}, u32[]{:S(2)}, u32[]{:S(2)}) collective-permute-start(bf16[8,16,1024]{2,1,0:T(8,128)(2,1)S(1)} %get-tuple-element.64), channel_id=1, source_target_pairs={{0,1},{1,2},{2,3},{3,0},{4,5},{5,6},{6,7},{7,4},{8,9},{9,10},{10,1... | collective-permute-start | bytes 786440 | tf_op jit(solution)/shard_map/ppermute | solution.py:308
  140.3 1.1 collective-permute-start.24
  141.3 1.1 collective-permute-done.21.h1
  142.4 4.9 %shard_map.72 = bf16[1024,1280]{1,0:T(8,128)(2,1)} custom-call(s32[4]{0:T(128)S(1)} %copy-done.3, bf16[512,1024]{1,0:T(8,128)(2,1)S(1)} %copy-done.5, bf16[512,1024]{1,0:T(8,128)(2,1)S(1)} %collective-permute-done.21.h1, bf16[512,1280]{1,0:T(8,128)(2,1)S(1)} %get-tuple-element.62.g0, bf16[512,1280]{1,0:T(8,128)(2,1)S(1)} %collective-permute-done.22.g1), custom_call_target="tpu_custom_call" | custom-call | flops 2684354560 | bytes 8388608 | tf_op jit(solution)/shard_map/pallas_call | solution.py:28
  147.4 4.4 %collective-permute-done.23 = bf16[8,16,1024]{2,1,0:T(8,128)(2,1)S(1)} collective-permute-done((bf16[8,16,1024]{2,1,0:T(8,128)(2,1)S(1)}, bf16[8,16,1024]{2,1,0:T(8,128)(2,1)S(1)}, u32[]{:S(2)}, u32[]{:S(2)}) %collective-permute-start.23) | collective-permute-done | bytes 262176 | tf_op jit(solution)/shard_map/ppermute | solution.py:308
  151.8 3.7 %collective-permute-done.25 = bf16[8,16,1024]{2,1,0:T(8,128)(2,1)S(1)} collective-permute-done((bf16[8,16,1024]{2,1,0:T(8,128)(2,1)S(1)}, bf16[8,16,1024]{2,1,0:T(8,128)(2,1)S(1)}, u32[]{:S(2)}, u32[]{:S(2)}) %collective-permute-start.25) | collective-permute-done | bytes 262176 | tf_op jit(solution)/shard_map/ppermute | solution.py:308
  155.4 0.9 add_convert_fusion
  156.3 4.5 %all-to-all-start.3 = ((bf16[8,16,1024]{2,1,0:T(8,128)(2,1)}), bf16[8,16,1024]{2,1,0:T(8,128)(2,1)S(1)}, u32[]{:S(2)}, u32[]{:S(2)}) async-start(bf16[8,16,1024]{2,1,0:T(8,128)(2,1)} %add_convert_fusion), calls=%async_computation.3 | async-start | bytes 524288 | tf_op jit(solution)/shard_map/all_to_all | solution.py:322
  160.8 0.7 slice.17
  161.7 1.0 collective-permute-done.15
  163.5 9.4 %all-to-all-done.3 = bf16[8,16,1024]{2,1,0:T(8,128)(2,1)S(1)} async-done(((bf16[8,16,1024]{2,1,0:T(8,128)(2,1)}), bf16[8,16,1024]{2,1,0:T(8,128)(2,1)S(1)}, u32[]{:S(2)}, u32[]{:S(2)}) %all-to-all-start.3) | async-done | bytes 262176 | tf_op jit(solution)/shard_map/all_to_all | solution.py:322
  172.9 0.7 reduce_sum.12
  (67 shorter events, 5.0 us)
Async XLA Ops:
  2.1 10.4 %all-to-all-start = ((bf16[4,16,1024]{2,1,0:T(8,128)(2,1)}), bf16[4,16,1024]{2,1,0:T(8,128)(2,1)S(1)}, u32[]{:S(2)}, u32[]{:S(2)}) async-start(bf16[4,16,1024]{2,1,0:T(8,128)(2,1)} %broadcast_in_dim.6), calls=%async_computation | async-start | bytes 262144 | tf_op jit(solution)/shard_map/all_to_all | solution.py:218
  6.5 53.1 %copy-start = (bf16[1024,1280]{1,0:T(8,128)(2,1)S(1)}, bf16[1024,1280]{1,0:T(8,128)(2,1)}, u32[]{:S(2)}) copy-start(bf16[1024,1280]{1,0:T(8,128)(2,1)} %own.1) | copy-start | bytes 7864324
  10.1 41.8 %copy-start.10 = (s32[1024]{0:T(1024)S(1)}, s32[1024]{0:T(1024)}, u32[]{:S(2)}) copy-start(s32[1024]{0:T(1024)} %param.6) | copy-start | bytes 12292
  10.1 42.0 %copy-start.11 = (f32[1024]{0:T(1024)S(1)}, f32[1024]{0:T(1024)}, u32[]{:S(2)}) copy-start(f32[1024]{0:T(1024)} %param.7) | copy-start | bytes 12292
  13.3 16.6 %all-to-all-start.1 = ((bf16[4,16,4096]{2,1,0:T(8,128)(2,1)}), bf16[4,16,4096]{2,1,0:T(8,128)(2,1)S(1)}, u32[]{:S(2)}, u32[]{:S(2)}) async-start(bf16[4,16,4096]{2,1,0:T(8,128)(2,1)} %broadcast_in_dim.15), calls=%async_computation.1 | async-start | bytes 1048576 | tf_op jit(solution)/shard_map/all_to_all | solution.py:218
  18.1 34.7 %collective-permute-start = (bf16[1024,640]{1,0:T(8,128)(2,1)}, bf16[1024,640]{1,0:T(8,128)(2,1)}, u32[]{:S(2)}, u32[]{:S(2)}) collective-permute-start(bf16[1024,640]{1,0:T(8,128)(2,1)} %get-tuple-element.37), channel_id=1, source_target_pairs={{0,0},{4,4},{8,16},{12,20},{16,8},{20,12},{24,24},{28,28},{1,1},{5... | collective-permute-start | bytes 3932168 | tf_op jit(solution)/shard_map/ppermute | solution.py:229
  29.4 23.5 %collective-permute-start.1 = (bf16[1024,640]{1,0:T(8,128)(2,1)}, bf16[1024,640]{1,0:T(8,128)(2,1)}, u32[]{:S(2)}, u32[]{:S(2)}) collective-permute-start(bf16[1024,640]{1,0:T(8,128)(2,1)} %get-tuple-element.38), channel_id=1, source_target_pairs={{0,4},{4,0},{8,20},{12,16},{16,12},{20,8},{24,28},{28,24},{1,5},{5... | collective-permute-start | bytes 3932168 | tf_op jit(solution)/shard_map/ppermute | solution.py:229
  30.0 22.2 %copy-start.7 = (bf16[4,16,4096]{2,1,0:T(8,128)(2,1)}, bf16[4,16,4096]{2,1,0:T(8,128)(2,1)S(1)}, u32[]{:S(2)}) copy-start(bf16[4,16,4096]{2,1,0:T(8,128)(2,1)S(1)} %all-to-all-done.1) | copy-start | bytes 1572868
  30.0 18.4 %collective-permute-start.2 = (bf16[64,4096]{1,0:T(8,128)(2,1)S(1)}, bf16[64,4096]{1,0:T(8,128)(2,1)}, u32[]{:S(2)}, u32[]{:S(2)}) collective-permute-start(bf16[64,4096]{1,0:T(8,128)(2,1)S(1)} %bitcast.13), channel_id=1, source_target_pairs={{0,32},{32,64},{64,96},{96,128},{128,160},{160,192},{192,224},{224... | collective-permute-start | bytes 1572872 | tf_op jit(solution)/shard_map/ppermute | solution.py:278
  31.9 16.5 %collective-permute-start.4 = (bf16[64,4096]{1,0:T(8,128)(2,1)S(1)}, bf16[64,4096]{1,0:T(8,128)(2,1)}, u32[]{:S(2)}, u32[]{:S(2)}) collective-permute-start(bf16[64,4096]{1,0:T(8,128)(2,1)S(1)} %bitcast.14), channel_id=1, source_target_pairs={{0,224},{32,0},{64,32},{96,64},{128,96},{160,128},{192,160},{224,1... | collective-permute-start | bytes 1572872 | tf_op jit(solution)/shard_map/ppermute | solution.py:278
  48.4 10.7 %collective-permute-start.3 = (bf16[64,4096]{1,0:T(8,128)(2,1)}, bf16[64,4096]{1,0:T(8,128)(2,1)}, u32[]{:S(2)}, u32[]{:S(2)}) collective-permute-start(bf16[64,4096]{1,0:T(8,128)(2,1)} %collective-permute-done.2.refs_4_), channel_id=1, source_target_pairs={{0,32},{32,64},{64,96},{96,128},{128,160},{160,192},{192,224},{224... | collective-permute-start | bytes 1572872 | tf_op jit(solution)/shard_map/ppermute | solution.py:278
  48.4 10.7 %collective-permute-start.5 = (bf16[64,4096]{1,0:T(8,128)(2,1)}, bf16[64,4096]{1,0:T(8,128)(2,1)}, u32[]{:S(2)}, u32[]{:S(2)}) collective-permute-start(bf16[64,4096]{1,0:T(8,128)(2,1)} %collective-permute-done.4.refs_1_), channel_id=1, source_target_pairs={{0,224},{32,0},{64,32},{96,64},{128,96},{160,128},{192,160},{224,1... | collective-permute-start | bytes 1572872 | tf_op jit(solution)/shard_map/ppermute | solution.py:278
  59.1 5.0 %collective-permute-start.6 = (bf16[1024,640]{1,0:T(8,128)(2,1)}, bf16[1024,640]{1,0:T(8,128)(2,1)}, u32[]{:S(2)}, u32[]{:S(2)}) collective-permute-start(bf16[1024,640]{1,0:T(8,128)(2,1)} %collective-permute-done.refs_5_.b0), channel_id=1, source_target_pairs={{0,16},{16,0},{1,17},{17,1},{2,18},{18,2},{3,19},{19,3},{4,20},{20... | collective-permute-start | bytes 3932168 | tf_op jit(solution)/shard_map/ppermute | solution.py:259
  59.1 7.1 %collective-permute-start.7 = (bf16[1024,640]{1,0:T(8,128)(2,1)}, bf16[1024,640]{1,0:T(8,128)(2,1)}, u32[]{:S(2)}, u32[]{:S(2)}) collective-permute-start(bf16[1024,640]{1,0:T(8,128)(2,1)} %collective-permute-done.1.refs_6_.b1), channel_id=1, source_target_pairs={{0,16},{16,0},{1,17},{17,1},{2,18},{18,2},{3,19},{19,3},{4,20},{20... | collective-permute-start | bytes 3932168 | tf_op jit(solution)/shard_map/ppermute | solution.py:259
  59.6 70.0 %collective-permute-start.20 = (bf16[1024,1280]{1,0:T(8,128)(2,1)S(1)}, bf16[1024,1280]{1,0:T(8,128)(2,1)}, u32[]{:S(2)}, u32[]{:S(2)}) collective-permute-start(bf16[1024,1280]{1,0:T(8,128)(2,1)S(1)} %copy-done), channel_id=1, source_target_pairs={{0,16},{16,0},{1,17},{17,1},{2,18},{18,2},{3,19},{19,3},{4,20},{20... | collective-permute-start | bytes 7864328 | tf_op jit(solution)/shard_map/ppermute | solution.py:260
  59.6 16.9 %collective-permute-start.8 = (bf16[64,4096]{1,0:T(8,128)(2,1)}, bf16[64,4096]{1,0:T(8,128)(2,1)S(1)}, u32[]{:S(2)}, u32[]{:S(2)}) collective-permute-start(bf16[64,4096]{1,0:T(8,128)(2,1)} %collective-permute-done.3.refs_3_), channel_id=1, source_target_pairs={{0,32},{32,64},{64,96},{96,128},{128,160},{160,192},{192,224},{224... | collective-permute-start | bytes 1572872 | tf_op jit(solution)/shard_map/ppermute | solution.py:278
  59.6 16.9 %collective-permute-start.9 = (bf16[64,4096]{1,0:T(8,128)(2,1)}, bf16[64,4096]{1,0:T(8,128)(2,1)}, u32[]{:S(2)}, u32[]{:S(2)}) collective-permute-start(bf16[64,4096]{1,0:T(8,128)(2,1)} %collective-permute-done.5.refs_2_), channel_id=1, source_target_pairs={{0,224},{32,0},{64,32},{96,64},{128,96},{160,128},{192,160},{224,1... | collective-permute-start | bytes 1572872 | tf_op jit(solution)/shard_map/ppermute | solution.py:278
  76.5 11.2 %copy-start.6 = (bf16[64,4096]{1,0:T(8,128)(2,1)}, bf16[64,4096]{1,0:T(8,128)(2,1)S(1)}, u32[]{:S(2)}) copy-start(bf16[64,4096]{1,0:T(8,128)(2,1)S(1)} %collective-permute-done.8.p5) | copy-start | bytes 1572868
  76.5 10.4 %collective-permute-start.10 = (bf16[32,4096]{1,0:T(8,128)(2,1)S(1)}, bf16[32,4096]{1,0:T(8,128)(2,1)S(1)}, u32[]{:S(2)}, u32[]{:S(2)}) collective-permute-start(bf16[32,4096]{1,0:T(8,128)(2,1)S(1)} %slice.15), channel_id=1, source_target_pairs={{0,32},{32,64},{64,96},{96,128},{128,160},{160,192},{192,224},{224... | collective-permute-start | bytes 786440 | tf_op jit(solution)/shard_map/ppermute | solution.py:278
  80.0 7.7 %collective-permute-start.11 = (bf16[32,4096]{1,0:T(8,128)(2,1)S(1)}, bf16[32,4096]{1,0:T(8,128)(2,1)S(1)}, u32[]{:S(2)}, u32[]{:S(2)}) collective-permute-start(bf16[32,4096]{1,0:T(8,128)(2,1)S(1)} %slice.16), channel_id=1, source_target_pairs={{0,224},{32,0},{64,32},{96,64},{128,96},{160,128},{192,160},{224,1... | collective-permute-start | bytes 786440 | tf_op jit(solution)/shard_map/ppermute | solution.py:278
  86.9 0.8 copy-start.8
  87.7 0.7 copy-start.9
  96.0 23.4 %copy-start.3 = (s32[4]{0:T(128)S(1)}, s32[4]{0:T(128)}, u32[]{:S(2)}) copy-start(s32[4]{0:T(128)} %pad_add_fusion.pos) | copy-start | bytes 52
  96.0 33.7 %copy-start.1 = (s32[512,1]{1,0:T(8,128)S(1)}, s32[512,1]{1,0:T(8,128)}, u32[]{:S(2)}) copy-start(s32[512,1]{1,0:T(8,128)} %copy.17.targets) | copy-start | bytes 6148
  96.0 17.7 %collective-permute-start.16 = (bf16[512,640]{1,0:T(8,128)(2,1)}, bf16[512,640]{1,0:T(8,128)(2,1)S(1)}, u32[]{:S(2)}, u32[]{:S(2)}) collective-permute-start(bf16[512,640]{1,0:T(8,128)(2,1)} %get-tuple-element.58.e0), channel_id=1, source_target_pairs={{0,4},{4,8},{8,12},{12,0},{1,5},{5,9},{9,13},{13,1},{2,6},{6,10},{... | collective-permute-start | bytes 1966088 | tf_op jit(solution)/shard_map/ppermute | solution.py:290
  97.3 17.2 %collective-permute-start.18 = (bf16[512,640]{1,0:T(8,128)(2,1)}, bf16[512,640]{1,0:T(8,128)(2,1)}, u32[]{:S(2)}, u32[]{:S(2)}) collective-permute-start(bf16[512,640]{1,0:T(8,128)(2,1)} %get-tuple-element.58.e0), channel_id=1, source_target_pairs={{0,12},{4,0},{8,4},{12,8},{1,13},{5,1},{9,5},{13,9},{2,14},{6,2},{... | collective-permute-start | bytes 1966088 | tf_op jit(solution)/shard_map/ppermute | solution.py:290
  99.3 20.1 %all-to-all-start.2 = ((f32[32,16,128]{2,1,0:T(8,128)}), f32[32,16,128]{2,1,0:T(8,128)}, u32[]{:S(2)}, u32[]{:S(2)}) async-start(f32[32,16,128]{2,1,0:T(8,128)} %get-tuple-element.54), calls=%async_computation.2 | async-start | bytes 524288 | tf_op jit(solution)/shard_map/all_to_all | solution.py:291
  114.4 15.2 %collective-permute-start.17 = (bf16[256,640]{1,0:T(8,128)(2,1)}, bf16[256,640]{1,0:T(8,128)(2,1)}, u32[]{:S(2)}, u32[]{:S(2)}) collective-permute-start(bf16[256,640]{1,0:T(8,128)(2,1)} %slice.20), channel_id=1, source_target_pairs={{0,4},{4,8},{8,12},{12,0},{1,5},{5,9},{9,13},{13,1},{2,6},{6,10},{... | collective-permute-start | bytes 983048 | tf_op jit(solution)/shard_map/ppermute | solution.py:292
  116.2 13.4 %collective-permute-start.19 = (bf16[256,640]{1,0:T(8,128)(2,1)}, bf16[256,640]{1,0:T(8,128)(2,1)}, u32[]{:S(2)}, u32[]{:S(2)}) collective-permute-start(bf16[256,640]{1,0:T(8,128)(2,1)} %slice.21), channel_id=1, source_target_pairs={{0,12},{4,0},{8,4},{12,8},{1,13},{5,1},{9,5},{13,9},{2,14},{6,2},{... | collective-permute-start | bytes 983048 | tf_op jit(solution)/shard_map/ppermute | solution.py:293
  120.4 4.9 %collective-permute-start.12 = (f32[16,128]{1,0:T(8,128)S(1)}, f32[16,128]{1,0:T(8,128)S(1)}, u32[]{:S(2)}, u32[]{:S(2)}) collective-permute-start(f32[16,128]{1,0:T(8,128)S(1)} %shard_map.69.t0), channel_id=1, source_target_pairs={{0,4},{4,8},{8,12},{12,0},{1,5},{5,9},{9,13},{13,1},{2,6},{6,10},{... | collective-permute-start | bytes 24584 | tf_op jit(solution)/shard_map/ppermute | solution.py:295
  120.5 5.2 %collective-permute-start.13 = (f32[16,128]{1,0:T(8,128)S(1)}, f32[16,128]{1,0:T(8,128)S(1)}, u32[]{:S(2)}, u32[]{:S(2)}) collective-permute-start(f32[16,128]{1,0:T(8,128)S(1)} %shard_map.69.t0), channel_id=1, source_target_pairs={{0,8},{4,12},{8,0},{12,4},{1,9},{5,13},{9,1},{13,5},{2,10},{6,14},... | collective-permute-start | bytes 24584 | tf_op jit(solution)/shard_map/ppermute | solution.py:295
  125.3 3.7 %collective-permute-start.14 = (f32[16,128]{1,0:T(8,128)S(1)}, f32[16,128]{1,0:T(8,128)S(1)}, u32[]{:S(2)}, u32[]{:S(2)}) collective-permute-start(f32[16,128]{1,0:T(8,128)S(1)} %shard_map.69.t0), channel_id=1, source_target_pairs={{0,12},{4,0},{8,4},{12,8},{1,13},{5,1},{9,5},{13,9},{2,14},{6,2},{... | collective-permute-start | bytes 24584 | tf_op jit(solution)/shard_map/ppermute | solution.py:295
  129.6 8.0 %copy-start.4 = (f32[8,512]{1,0:T(8,128)}, f32[8,512]{1,0:T(8,128)S(1)}, u32[]{:S(2)}) copy-start(f32[8,512]{1,0:T(8,128)S(1)} %get-tuple-element.56) | copy-start | bytes 49156
  129.6 1.1 copy-start.2
  130.7 7.1 %copy-start.5 = (bf16[512,1024]{1,0:T(8,128)(2,1)S(1)}, bf16[512,1024]{1,0:T(8,128)(2,1)}, u32[]{:S(2)}) copy-start(bf16[512,1024]{1,0:T(8,128)(2,1)} %get-tuple-element.61.h0) | copy-start | bytes 3145732
  137.6 4.8 %collective-permute-start.22 = (bf16[512,1280]{1,0:T(8,128)(2,1)S(1)}, bf16[512,1280]{1,0:T(8,128)(2,1)S(1)}, u32[]{:S(2)}, u32[]{:S(2)}) collective-permute-start(bf16[512,1280]{1,0:T(8,128)(2,1)S(1)} %get-tuple-element.63), channel_id=1, source_target_pairs={{0,16},{16,0},{1,17},{17,1},{2,18},{18,2},{3,19},{19,3},{4,20},{20... | collective-permute-start | bytes 3932168 | tf_op jit(solution)/shard_map/ppermute | solution.py:309
  137.9 4.5 %collective-permute-start.21 = (bf16[512,1024]{1,0:T(8,128)(2,1)S(1)}, bf16[512,1024]{1,0:T(8,128)(2,1)S(1)}, u32[]{:S(2)}, u32[]{:S(2)}) collective-permute-start(bf16[512,1024]{1,0:T(8,128)(2,1)S(1)} %copy-done.5), channel_id=1, source_target_pairs={{0,16},{16,0},{1,17},{17,1},{2,18},{18,2},{3,19},{19,3},{4,20},{20... | collective-permute-start | bytes 3145736 | tf_op jit(solution)/shard_map/ppermute | solution.py:297
  138.4 13.4 %collective-permute-start.23 = (bf16[8,16,1024]{2,1,0:T(8,128)(2,1)S(1)}, bf16[8,16,1024]{2,1,0:T(8,128)(2,1)S(1)}, u32[]{:S(2)}, u32[]{:S(2)}) collective-permute-start(bf16[8,16,1024]{2,1,0:T(8,128)(2,1)S(1)} %get-tuple-element.64), channel_id=1, source_target_pairs={{0,1},{1,2},{2,3},{3,0},{4,5},{5,6},{6,7},{7,4},{8,9},{9,10},{10,1... | collective-permute-start | bytes 786440 | tf_op jit(solution)/shard_map/ppermute | solution.py:308
  140.3 11.5 %collective-permute-start.24 = (bf16[8,16,1024]{2,1,0:T(8,128)(2,1)S(1)}, bf16[8,16,1024]{2,1,0:T(8,128)(2,1)S(1)}, u32[]{:S(2)}, u32[]{:S(2)}) collective-permute-start(bf16[8,16,1024]{2,1,0:T(8,128)(2,1)S(1)} %get-tuple-element.65), channel_id=1, source_target_pairs={{0,2},{1,3},{2,0},{3,1},{4,6},{5,7},{6,4},{7,5},{8,10},{9,11},{10,... | collective-permute-start | bytes 786440 | tf_op jit(solution)/shard_map/ppermute | solution.py:308
  141.3 14.1 %collective-permute-start.25 = (bf16[8,16,1024]{2,1,0:T(8,128)(2,1)S(1)}, bf16[8,16,1024]{2,1,0:T(8,128)(2,1)S(1)}, u32[]{:S(2)}, u32[]{:S(2)}) collective-permute-start(bf16[8,16,1024]{2,1,0:T(8,128)(2,1)S(1)} %get-tuple-element.66), channel_id=1, source_target_pairs={{0,3},{1,0},{2,1},{3,2},{4,7},{5,4},{6,5},{7,6},{8,11},{9,8},{10,9... | collective-permute-start | bytes 786440 | tf_op jit(solution)/shard_map/ppermute | solution.py:308
  156.3 16.6 %all-to-all-start.3 = ((bf16[8,16,1024]{2,1,0:T(8,128)(2,1)}), bf16[8,16,1024]{2,1,0:T(8,128)(2,1)S(1)}, u32[]{:S(2)}, u32[]{:S(2)}) async-start(bf16[8,16,1024]{2,1,0:T(8,128)(2,1)} %add_convert_fusion), calls=%async_computation.3 | async-start | bytes 524288 | tf_op jit(solution)/shard_map/all_to_all | solution.py:322
  161.5 1.2 collective-permute-start.15

commit v3 on v2

--- a/solution.py
+++ b/solution.py
@@ -36,66 +36,42 @@
     )(*args)
 
 
-def early_kernel(count, pos, targets, *refs):
+def rows_kernel(aheads, count, first, last, pos, targets, *refs):
+    refs = list(refs)
+    before = [] if first else [refs.pop(0) for _ in range(3)]
     pieces, blocks = refs[:count], refs[count : count + 4]
-    e_out, table_out, slice_out, acc, hid_v, block_v, hid_sem, block_sem = refs[count + 4 :]
+    e_out, slice_out, third = refs[count + 4 : count + 7]
+    rest = refs[count + 7 :]
+    table = rest.pop(0) if last else third
+    acc, hid_v, block_v, hid_sem, block_sem = rest
     z, c, y, x = (pos[i] for i in range(4))
-    _, width, group = block_v.shape
-    per_z = pieces[0].shape[0]
+    width = block_v.shape[1]
+    per_z, size = hid_v.shape[0] // len(aheads), hid_v.shape[0] // count
+    copies = [
+        pltpu.make_async_copy(p, hid_v.at[pl.ds(i * size, size)], hid_sem.at[i])
+        for i, p in enumerate(pieces)
+    ]
     block_copies = [
         pltpu.make_async_copy(b, block_v.at[i], block_sem.at[i]) for i, b in enumerate(blocks)
     ]
-    copies = []
-    for i, p in enumerate(pieces):
-        first = lax.rem(z + i + 3 * (i > 2), NZ) * per_z
-        at = pl.ds(pl.multiple_of(first, 64), per_z)
-        copies.append(pltpu.make_async_copy(p, hid_v.at[at], hid_sem.at[i]))
     for copy in copies + block_copies:
         copy.start()
-    for ahead in (3, 4, 5):
-        hid_v[pl.ds(pl.multiple_of(lax.rem(z + ahead, NZ) * per_z, 64), per_z)] = jnp.zeros(
-            (per_z, hid_v.shape[1]), BF16
-        )
-    for copy in copies:
-        copy.wait()
-    multiply(hid_v, block_v, block_copies, acc, c, y)
-    slice_out[...] = columns(hid_v, y, width)
-    e_out[...], table_out[...] = soften(acc[...], targets[...], z, y, x)
-
-
-def late_kernel(pos, targets, e_in, table_in, slice_in, p3, p5, p4a, p4b, b0, b1, b2, b3, *refs):
-    e_out, slice_out, stats_out, table, acc, hid_v, block_v, hid_sem, block_sem = refs
-    z, c, y, x = (pos[i] for i in range(4))
-    _, width, group = block_v.shape
-    per_z = p3.shape[0]
-    block_copies = [
-        pltpu.make_async_copy(b, block_v.at[i], block_sem.at[i])
-        for i, b in enumerate((b0, b1, b2, b3))
-    ]
-    copies = [
-        pltpu.make_async_copy(p, hid_v.at[pl.ds(first, p.shape[0])], hid_sem.at[i])
-        for i, (p, first) in enumerate(
-            ((p3, 0), (p4a, per_z), (p4b, per_z + per_z // 2), (p5, 2 * per_z))
-        )
-    ]
-    for copy in copies + block_copies:
-        copy.start()
-    e_out[...] = e_in[...]
-    slice_out[...] = slice_in[...]
-    table[...] = table_in[...]
+    for old, new in zip(before, (e_out, slice_out, table)):
+        new[...] = old[...]
     for copy in copies:
         copy.wait()
     multiply(hid_v, block_v, block_copies, acc, c, y)
     mine = columns(hid_v, y, width)
-    for i in range(3):
+    for i, ahead in enumerate(aheads):
         part = slice(i * per_z, (i + 1) * per_z)
-        here = pl.ds(pl.multiple_of(lax.rem(z + 3 + i, NZ) * per_z, 64), per_z)
+        here = pl.ds(pl.multiple_of(lax.rem(z + ahead, NZ) * per_z, 64), per_z)
         slice_out[here] = mine[part]
         e_out[here], table[here] = soften(acc[part], targets[here], z, y, x)
-    flat = table[...].T
-    packed = pack([flat[0:1], flat[1:2], flat[2:3]])
-    for i in range(stats_out.shape[0]):
-        stats_out[i] = packed
+    if last:
+        flat = table[...].T
+        packed = pack([flat[0:1], flat[1:2], flat[2:3]])
+        for i in range(third.shape[0]):
+            third[i] = packed
 
 
 def columns(hid_v, origin, width):
@@ -240,14 +216,26 @@
     my_targets, my_weights = ordered(targets)[:, None], ordered(weights)[None]
 
     size = NZ * per_z
-    def scratch(rows, pieces):
-        return [
-            pltpu.VMEM((rows, group), F32),
-            pltpu.VMEM((rows, NY * width), BF16),
-            pltpu.VMEM((NY, width, group), BF16),
-            pltpu.SemaphoreType.DMA((pieces,)),
-            pltpu.SemaphoreType.DMA((NY,)),
-        ]
+    def logits_stage(aheads, pieces, before=(), last=False):
+        count, held = len(pieces), len(aheads) * per_z
+        third = ((NZ * NX, 16, 128), F32) if last else ((size, 128), F32)
+        return call(
+            functools.partial(rows_kernel, aheads, count, not before, last),
+            [((size, group), BF16), ((size, width), BF16), third],
+            (pos, my_targets, *before, *pieces, *blocks),
+            scratch=[pltpu.VMEM((size, 128), F32)] * last
+            + [
+                pltpu.VMEM((held, group), F32),
+                pltpu.VMEM((held, NY * width), BF16),
+                pltpu.VMEM((NY, width, group), BF16),
+                pltpu.SemaphoreType.DMA((count,)),
+                pltpu.SemaphoreType.DMA((NY,)),
+            ],
+            far=count + 4,
+            vmem=56 if before else 60,
+            flops=1000 if last else 2 * size * NY * width * group,
+            moved=1000 if last else 10 * 2**20,
+        )
 
     pieces, flying = {0: near}, {1: near, -1: near}
     for step in range(1, 5):
@@ -260,17 +248,7 @@
             other = lax.ppermute(head_later, "core", SWAP)
         if step == 4:
             blocks = (got0, got1, twin0, twin1)
-            hid = [pieces[r] for r in (0, 1, 2, 6, 7)]
-            e, table, mine = call(
-                functools.partial(early_kernel, len(hid)),
-                [((size, group), BF16), ((size, 128), F32), ((size, width), BF16)],
-                (pos, my_targets, *hid, *blocks),
-                scratch=scratch(size, len(hid)),
-                far=len(hid) + 4,
-                vmem=60,
-                flops=2 * size * NY * width * group,
-                moved=10 * 2**20,
-            )
+            e, mine, table = logits_stage((0, 1, 2, 6, 7), [pieces[r] for r in (0, 1, 2, 6, 7)])
             e, table, mine, *tied = tie(e, table, mine, flying[1], flying[-1])
             flying = {1: tied[0], -1: tied[1]}
             flying = {1: flying[1][: per_z // 2], -1: flying[-1][per_z // 2 :]}
@@ -278,14 +256,8 @@
             flying[d] = lax.ppermute(flying[d], "z", shift(NZ, d))
             pieces[-d * step if step == 4 else (-d * step) % NZ] = flying[d]
 
-    e, mine, stats = call(
-        late_kernel,
-        [((size, group), BF16), ((size, width), BF16), ((NZ * NX, 16, 128), F32)],
-        (pos, my_targets, e, table, mine, *[pieces[r] for r in (3, 5, -4, 4)], *blocks),
-        scratch=[pltpu.VMEM((size, 128), F32)] + scratch(3 * per_z, 4),
-        far=8,
-        vmem=56,
-    )
+    e, mine, table = logits_stage((3, 5), [pieces[3], pieces[5]], (e, mine, table))
+    e, mine, stats = logits_stage((4,), [pieces[-4], pieces[4]], (e, mine, table), last=True)
 
     e1, e3 = lax.ppermute(e, "y", shift(NY, 1)), lax.ppermute(e, "y", shift(NY, -1))
     far = lax.all_to_all(stats, ("z", "x"), 0, 0, tiled=True)

time: 175 us -> 175 us (level)
  waiting for transfers between devices: 61 us -> 55.7 us
  Pallas kernels: 31.2 us -> 35.8 us
    ppermute x8, waiting for transfers between devices: 25.1 us -> 19.7 us  [body(): flying[d] = lax.ppermute(flying[d], 'z', shift(NZ, d))]
    pallas_call x6 -> x7, Pallas kernels: 31.2 us -> 35.8 us  [call(): pl.pallas_call(kernel, out_shape=[jax.ShapeDtypeStruct(s, d) for s, d in...]
  transfers between devices with their start and end apart: 30 -> 30, of which waited for: 15 -> 16; matrix products, arithmetic and copies ran while one was open for 6% -> 7% of each run, Pallas kernels for 14% -> 17%
where the time goes in v3:
time: 175 us; the launch traced here: 173 us
  starting transfers between devices  63.6 us (36%)
  waiting for transfers between devices  55.7 us (32%)
  Pallas kernels  35.8 us (20%)
  local copies, waits for them, and re-layouts  14.9 us (9%)
  other arithmetic  2.16 us (1%)
    pallas_call x7, Pallas kernels, call(): pl.pallas_call(kernel, out_shape=[jax.ShapeDtypeStruct(s, d) for s, d in...  35.8 us
    ppermute x8, waiting for transfers between devices, body(): flying[d] = lax.ppermute(flying[d], 'z', shift(NZ, d))  19.7 us
    ppermute x8, starting transfers between devices, body(): flying[d] = lax.ppermute(flying[d], 'z', shift(NZ, d))  16.6 us
    ppermute x2, starting transfers between devices, hand_over(): return lax.ppermute(v, ('core', 'y'), perm)  11.8 us
    all_to_all x1, waiting for transfers between devices, body(): got = lax.all_to_all(total, 'z', 0, 0, tiled=True)  9.38 us
    all_to_all x2, starting transfers between devices, copies(): return lax.all_to_all(flat, axis, 0, 0, tiled=True).reshape((n,) + v.shape)  9.23 us
    all_to_all x1, starting transfers between devices, body(): far = lax.all_to_all(stats, ('z', 'x'), 0, 0, tiled=True)  8.95 us
    ppermute x3, waiting for transfers between devices, body(): terms = [lax.ppermute(v, 'x', shift(NX, d + 1)) for d, v in enumerate(send)]  7.71 us
  transfers between devices with their start and end apart: 30, of which 16 were waited for; matrix products, arithmetic and copies ran while one was open for 7% of the time, Pallas kernels for 17%

profile of v3, /device:TPU:6, one launch (start us, length us, event | category | flops | bytes accessed | tf_op | source)
XLA Modules:
  0.0 173.0 jit_solution(3100600135977119016)
XLA Ops:
  0.6 1.4 broadcast_in_dim.6
  2.1 4.5 %all-to-all-start = ((bf16[4,16,1024]{2,1,0:T(8,128)(2,1)}), bf16[4,16,1024]{2,1,0:T(8,128)(2,1)S(1)}, u32[]{:S(2)}, u32[]{:S(2)}) async-start(bf16[4,16,1024]{2,1,0:T(8,128)(2,1)} %broadcast_in_dim.6), calls=%async_computation | async-start | bytes 262144 | tf_op jit(solution)/shard_map/all_to_all | solution.py:194
  6.5 3.6 %constant_dynamic-slice_fusion.1 = (bf16[1024,640]{1,0:T(8,128)(2,1)}, bf16[1024,640]{1,0:T(8,128)(2,1)}) fusion(bf16[1024,1280]{1,0:T(8,128)(2,1)} %own.1, s32[]{:T(128)S(6)} %select_n.39, s32[]{:T(128)S(6)} %select_n.37), kind=kLoop, calls=%fused_computation.6 | loop fusion | bytes 5242888 | tf_op jit(solution)/shard_map/dynamic_slice | solution.py:199
  10.1 2.4 %all-to-all-done = bf16[4,16,1024]{2,1,0:T(8,128)(2,1)S(1)} async-done(((bf16[4,16,1024]{2,1,0:T(8,128)(2,1)}), bf16[4,16,1024]{2,1,0:T(8,128)(2,1)S(1)}, u32[]{:S(2)}, u32[]{:S(2)}) %all-to-all-start) | async-done | bytes 131104 | tf_op jit(solution)/shard_map/all_to_all | solution.py:194
  12.5 0.8 broadcast_in_dim.15
  13.3 4.8 %all-to-all-start.1 = ((bf16[4,16,4096]{2,1,0:T(8,128)(2,1)}), bf16[4,16,4096]{2,1,0:T(8,128)(2,1)S(1)}, u32[]{:S(2)}, u32[]{:S(2)}) async-start(bf16[4,16,4096]{2,1,0:T(8,128)(2,1)} %broadcast_in_dim.15), calls=%async_computation.1 | async-start | bytes 1048576 | tf_op jit(solution)/shard_map/all_to_all | solution.py:194
  18.1 11.3 %collective-permute-start = (bf16[1024,640]{1,0:T(8,128)(2,1)}, bf16[1024,640]{1,0:T(8,128)(2,1)}, u32[]{:S(2)}, u32[]{:S(2)}) collective-permute-start(bf16[1024,640]{1,0:T(8,128)(2,1)} %get-tuple-element.40), channel_id=1, source_target_pairs={{0,0},{4,4},{8,16},{12,20},{16,8},{20,12},{24,24},{28,28},{1,1},{5... | collective-permute-start | bytes 3932168 | tf_op jit(solution)/shard_map/ppermute | solution.py:205
  30.0 1.9 %collective-permute-start.2 = (bf16[64,4096]{1,0:T(8,128)(2,1)S(1)}, bf16[64,4096]{1,0:T(8,128)(2,1)}, u32[]{:S(2)}, u32[]{:S(2)}) collective-permute-start(bf16[64,4096]{1,0:T(8,128)(2,1)S(1)} %bitcast.13), channel_id=1, source_target_pairs={{0,32},{32,64},{64,96},{96,128},{128,160},{160,192},{192,224},{224... | collective-permute-start | bytes 1572872 | tf_op jit(solution)/shard_map/ppermute | solution.py:256
  31.9 4.0 %collective-permute-start.4 = (bf16[64,4096]{1,0:T(8,128)(2,1)S(1)}, bf16[64,4096]{1,0:T(8,128)(2,1)}, u32[]{:S(2)}, u32[]{:S(2)}) collective-permute-start(bf16[64,4096]{1,0:T(8,128)(2,1)S(1)} %bitcast.14), channel_id=1, source_target_pairs={{0,224},{32,0},{64,32},{96,64},{128,96},{160,128},{192,160},{224,1... | collective-permute-start | bytes 1572872 | tf_op jit(solution)/shard_map/ppermute | solution.py:256
  35.9 12.5 %collective-permute-done.2.refs_4_ = bf16[64,4096]{1,0:T(8,128)(2,1)} collective-permute-done((bf16[64,4096]{1,0:T(8,128)(2,1)S(1)}, bf16[64,4096]{1,0:T(8,128)(2,1)}, u32[]{:S(2)}, u32[]{:S(2)}) %collective-permute-start.2) | collective-permute-done | bytes 524320 | tf_op jit(solution)/shard_map/ppermute | solution.py:256
  48.4 3.5 %collective-permute-start.5 = (bf16[64,4096]{1,0:T(8,128)(2,1)}, bf16[64,4096]{1,0:T(8,128)(2,1)}, u32[]{:S(2)}, u32[]{:S(2)}) collective-permute-start(bf16[64,4096]{1,0:T(8,128)(2,1)} %collective-permute-done.4.refs_1_), channel_id=1, source_target_pairs={{0,224},{32,0},{64,32},{96,64},{128,96},{160,128},{192,160},{224,1... | collective-permute-start | bytes 1572872 | tf_op jit(solution)/shard_map/ppermute | solution.py:256
  52.9 6.2 %collective-permute-done.3.refs_3_ = bf16[64,4096]{1,0:T(8,128)(2,1)} collective-permute-done((bf16[64,4096]{1,0:T(8,128)(2,1)}, bf16[64,4096]{1,0:T(8,128)(2,1)}, u32[]{:S(2)}, u32[]{:S(2)}) %collective-permute-start.3) | collective-permute-done | bytes 524320 | tf_op jit(solution)/shard_map/ppermute | solution.py:256
  59.6 3.6 %collective-permute-start.9 = (bf16[64,4096]{1,0:T(8,128)(2,1)}, bf16[64,4096]{1,0:T(8,128)(2,1)}, u32[]{:S(2)}, u32[]{:S(2)}) collective-permute-start(bf16[64,4096]{1,0:T(8,128)(2,1)} %collective-permute-done.5.refs_2_), channel_id=1, source_target_pairs={{0,224},{32,0},{64,32},{96,64},{128,96},{160,128},{192,160},{224,1... | collective-permute-start | bytes 1572872 | tf_op jit(solution)/shard_map/ppermute | solution.py:256
  63.2 0.9 copy.20.targets
  64.1 2.1 %collective-permute-done.7.refs_8_ = bf16[1024,640]{1,0:T(8,128)(2,1)} collective-permute-done((bf16[1024,640]{1,0:T(8,128)(2,1)}, bf16[1024,640]{1,0:T(8,128)(2,1)}, u32[]{:S(2)}, u32[]{:S(2)}) %collective-permute-start.7) | collective-permute-done | bytes 1310752 | tf_op jit(solution)/shard_map/ppermute | solution.py:247
  66.2 8.8 %shard_map.67 = (bf16[512,640]{1,0:T(8,128)(2,1)}, bf16[512,1024]{1,0:T(8,128)(2,1)}, f32[512,128]{1,0:T(8,128)}) custom-call(s32[4]{0:T(128)} %pad_add_fusion.pos, s32[512,1]{1,0:T(8,128)} %copy.20.targets, bf16[64,4096]{1,0:T(8,128)(2,1)} %bitcast.15, bf16[64,4096]{1,0:T(8,128)(2,1)} %collective-permute-done.4.refs_1_, ...), custom_call_target="tpu_custom_call" | custom-call | flops 2684354560 | bytes 10485760 | tf_op jit(solution)/shard_map/pallas_call | solution.py:28
  75.1 1.0 collective-permute-done.8.refs_4_
  76.0 1.0 slice.15
  77.0 2.7 %collective-permute-start.10 = (bf16[32,4096]{1,0:T(8,128)(2,1)S(1)}, bf16[32,4096]{1,0:T(8,128)(2,1)S(1)}, u32[]{:S(2)}, u32[]{:S(2)}) collective-permute-start(bf16[32,4096]{1,0:T(8,128)(2,1)S(1)} %slice.15), channel_id=1, source_target_pairs={{0,32},{32,64},{64,96},{96,128},{128,160},{160,192},{192,224},{224... | collective-permute-start | bytes 786440 | tf_op jit(solution)/shard_map/ppermute | solution.py:256
  79.8 1.0 slice.16
  80.7 0.8 collective-permute-start.11
  81.5 7.0 %shard_map.68 = (bf16[512,640]{1,0:T(8,128)(2,1)}, bf16[512,1024]{1,0:T(8,128)(2,1)}, f32[512,128]{1,0:T(8,128)}) custom-call(s32[4]{0:T(128)} %pad_add_fusion.pos, s32[512,1]{1,0:T(8,128)} %copy.20.targets, bf16[512,640]{1,0:T(8,128)(2,1)} %get-tuple-element.52.refs_0_, bf16[512,1024]{1,0:T(8,128)(2,1)} %get-tuple-element.53.refs_1_, ...), custom_call_target="tpu_custom_call" | custom-call | flops 2684354560 | bytes 10485760 | tf_op jit(solution)/shard_map/pallas_call | solution.py:28
  89.4 6.6 %shard_map.69 = (bf16[512,640]{1,0:T(8,128)(2,1)}, bf16[512,1024]{1,0:T(8,128)(2,1)}, f32[32,16,128]{2,1,0:T(8,128)}) custom-call(s32[4]{0:T(128)} %pad_add_fusion.pos, s32[512,1]{1,0:T(8,128)} %copy.20.targets, bf16[512,640]{1,0:T(8,128)(2,1)} %get-tuple-element.55.refs_0_, bf16[512,1024]{1,0:T(8,128)(2,1)} %get-tuple-element.56.refs_1_, ...), custom_call_target="tpu_custom_call" | custom-call | flops 1000 | bytes 1000 | tf_op jit(solution)/shard_map/pallas_call | solution.py:28
  96.0 1.4 collective-permute-start.16
  97.4 1.9 %collective-permute-start.18 = (bf16[512,640]{1,0:T(8,128)(2,1)}, bf16[512,640]{1,0:T(8,128)(2,1)}, u32[]{:S(2)}, u32[]{:S(2)}) collective-permute-start(bf16[512,640]{1,0:T(8,128)(2,1)} %get-tuple-element.64.e0), channel_id=1, source_target_pairs={{0,12},{4,0},{8,4},{12,8},{1,13},{5,1},{9,5},{13,9},{2,14},{6,2},{... | collective-permute-start | bytes 1966088 | tf_op jit(solution)/shard_map/ppermute | solution.py:262
  99.3 9.0 %all-to-all-start.2 = ((f32[32,16,128]{2,1,0:T(8,128)}), f32[32,16,128]{2,1,0:T(8,128)}, u32[]{:S(2)}, u32[]{:S(2)}) async-start(f32[32,16,128]{2,1,0:T(8,128)} %get-tuple-element.60), calls=%async_computation.2 | async-start | bytes 524288 | tf_op jit(solution)/shard_map/all_to_all | solution.py:263
  108.3 5.2 %collective-permute-done.16.e1 = bf16[512,640]{1,0:T(8,128)(2,1)S(1)} collective-permute-done((bf16[512,640]{1,0:T(8,128)(2,1)}, bf16[512,640]{1,0:T(8,128)(2,1)S(1)}, u32[]{:S(2)}, u32[]{:S(2)}) %collective-permute-start.16) | collective-permute-done | bytes 655392 | tf_op jit(solution)/shard_map/ppermute | solution.py:262
  113.5 0.8 slice.20
  114.4 1.7 %slice.21 = bf16[256,640]{1,0:T(8,128)(2,1)} slice(bf16[512,640]{1,0:T(8,128)(2,1)} %collective-permute-done.18.e3), slice={[256:512], [0:640]} | slice | bytes 655360 | tf_op jit(solution)/shard_map/slice | solution.py:265
  116.1 3.1 %collective-permute-start.19 = (bf16[256,640]{1,0:T(8,128)(2,1)}, bf16[256,640]{1,0:T(8,128)(2,1)}, u32[]{:S(2)}, u32[]{:S(2)}) collective-permute-start(bf16[256,640]{1,0:T(8,128)(2,1)} %slice.21), channel_id=1, source_target_pairs={{0,12},{4,0},{8,4},{12,8},{1,13},{5,1},{9,5},{13,9},{2,14},{6,2},{... | collective-permute-start | bytes 983048 | tf_op jit(solution)/shard_map/ppermute | solution.py:265
  119.2 1.0 shard_map.70.t0
  120.4 1.5 collective-permute-start.13
  121.8 3.4 %collective-permute-done.12.t1 = f32[16,128]{1,0:T(8,128)S(1)} collective-permute-done((f32[16,128]{1,0:T(8,128)S(1)}, f32[16,128]{1,0:T(8,128)S(1)}, u32[]{:S(2)}, u32[]{:S(2)}) %collective-permute-start.12) | collective-permute-done | bytes 8224 | tf_op jit(solution)/shard_map/ppermute | solution.py:267
  125.6 3.3 %collective-permute-done.14.t3 = f32[16,128]{1,0:T(8,128)S(1)} collective-permute-done((f32[16,128]{1,0:T(8,128)S(1)}, f32[16,128]{1,0:T(8,128)S(1)}, u32[]{:S(2)}, u32[]{:S(2)}) %collective-permute-start.14) | collective-permute-done | bytes 8224 | tf_op jit(solution)/shard_map/ppermute | solution.py:267
  129.5 1.1 copy-done.2
  130.6 6.8 %shard_map.72 = (bf16[512,1280]{1,0:T(8,128)(2,1)S(1)}, bf16[512,1280]{1,0:T(8,128)(2,1)S(1)}, f32[8,16,1024]{2,1,0:T(8,128)S(1)}, bf16[8,16,1024]{2,1,0:T(8,128...) custom-call(s32[4]{0:T(128)S(1)} %copy-done.3, s32[512,1]{1,0:T(8,128)S(1)} %copy-done.1, ...), custom_call_target="tpu_custom_call" | custom-call | flops 1000 | bytes 1000 | tf_op jit(solution)/shard_map/pallas_call | solution.py:28
  138.2 1.5 collective-permute-start.23
  139.8 1.4 collective-permute-start.24
  141.2 1.1 collective-permute-done.21.h1
  142.3 4.9 %shard_map.73 = bf16[1024,1280]{1,0:T(8,128)(2,1)} custom-call(s32[4]{0:T(128)S(1)} %copy-done.3, bf16[512,1024]{1,0:T(8,128)(2,1)S(1)} %copy-done.5, bf16[512,1024]{1,0:T(8,128)(2,1)S(1)} %collective-permute-done.21.h1, bf16[512,1280]{1,0:T(8,128)(2,1)S(1)} %get-tuple-element.68.g0, bf16[512,1280]{1,0:T(8,128)(2,1)S(1)} %collective-permute-done.22.g1), custom_call_target="tpu_custom_call" | custom-call | flops 2684354560 | bytes 8388608 | tf_op jit(solution)/shard_map/pallas_call | solution.py:28
  147.4 3.1 %collective-permute-done.24 = bf16[8,16,1024]{2,1,0:T(8,128)(2,1)S(1)} collective-permute-done((bf16[8,16,1024]{2,1,0:T(8,128)(2,1)S(1)}, bf16[8,16,1024]{2,1,0:T(8,128)(2,1)S(1)}, u32[]{:S(2)}, u32[]{:S(2)}) %collective-permute-start.24) | collective-permute-done | bytes 262176 | tf_op jit(solution)/shard_map/ppermute | solution.py:280
  150.5 4.4 %collective-permute-done.25 = bf16[8,16,1024]{2,1,0:T(8,128)(2,1)S(1)} collective-permute-done((bf16[8,16,1024]{2,1,0:T(8,128)(2,1)S(1)}, bf16[8,16,1024]{2,1,0:T(8,128)(2,1)S(1)}, u32[]{:S(2)}, u32[]{:S(2)}) %collective-permute-start.25) | collective-permute-done | bytes 262176 | tf_op jit(solution)/shard_map/ppermute | solution.py:280
  154.9 0.9 add_convert_fusion
  155.8 4.5 %all-to-all-start.3 = ((bf16[8,16,1024]{2,1,0:T(8,128)(2,1)}), bf16[8,16,1024]{2,1,0:T(8,128)(2,1)S(1)}, u32[]{:S(2)}, u32[]{:S(2)}) async-start(bf16[8,16,1024]{2,1,0:T(8,128)(2,1)} %add_convert_fusion), calls=%async_computation.3 | async-start | bytes 524288 | tf_op jit(solution)/shard_map/all_to_all | solution.py:294
  160.3 0.7 slice.17
  161.2 1.0 collective-permute-done.15
  163.0 9.4 %all-to-all-done.3 = bf16[8,16,1024]{2,1,0:T(8,128)(2,1)S(1)} async-done(((bf16[8,16,1024]{2,1,0:T(8,128)(2,1)}), bf16[8,16,1024]{2,1,0:T(8,128)(2,1)S(1)}, u32[]{:S(2)}, u32[]{:S(2)}) %all-to-all-start.3) | async-done | bytes 262176 | tf_op jit(solution)/shard_map/all_to_all | solution.py:294
  172.4 0.7 reduce_sum.12
  (66 shorter events, 6.0 us)
Async XLA Ops:
  2.1 10.4 %all-to-all-start = ((bf16[4,16,1024]{2,1,0:T(8,128)(2,1)}), bf16[4,16,1024]{2,1,0:T(8,128)(2,1)S(1)}, u32[]{:S(2)}, u32[]{:S(2)}) async-start(bf16[4,16,1024]{2,1,0:T(8,128)(2,1)} %broadcast_in_dim.6), calls=%async_computation | async-start | bytes 262144 | tf_op jit(solution)/shard_map/all_to_all | solution.py:194
  6.5 53.1 %copy-start = (bf16[1024,1280]{1,0:T(8,128)(2,1)S(1)}, bf16[1024,1280]{1,0:T(8,128)(2,1)}, u32[]{:S(2)}) copy-start(bf16[1024,1280]{1,0:T(8,128)(2,1)} %own.1) | copy-start | bytes 7864324
  10.1 41.8 %copy-start.9 = (s32[1024]{0:T(1024)S(1)}, s32[1024]{0:T(1024)}, u32[]{:S(2)}) copy-start(s32[1024]{0:T(1024)} %param.6) | copy-start | bytes 12292
  10.1 42.0 %copy-start.10 = (f32[1024]{0:T(1024)S(1)}, f32[1024]{0:T(1024)}, u32[]{:S(2)}) copy-start(f32[1024]{0:T(1024)} %param.7) | copy-start | bytes 12292
  13.3 16.6 %all-to-all-start.1 = ((bf16[4,16,4096]{2,1,0:T(8,128)(2,1)}), bf16[4,16,4096]{2,1,0:T(8,128)(2,1)S(1)}, u32[]{:S(2)}, u32[]{:S(2)}) async-start(bf16[4,16,4096]{2,1,0:T(8,128)(2,1)} %broadcast_in_dim.15), calls=%async_computation.1 | async-start | bytes 1048576 | tf_op jit(solution)/shard_map/all_to_all | solution.py:194
  18.1 34.8 %collective-permute-start = (bf16[1024,640]{1,0:T(8,128)(2,1)}, bf16[1024,640]{1,0:T(8,128)(2,1)}, u32[]{:S(2)}, u32[]{:S(2)}) collective-permute-start(bf16[1024,640]{1,0:T(8,128)(2,1)} %get-tuple-element.40), channel_id=1, source_target_pairs={{0,0},{4,4},{8,16},{12,20},{16,8},{20,12},{24,24},{28,28},{1,1},{5... | collective-permute-start | bytes 3932168 | tf_op jit(solution)/shard_map/ppermute | solution.py:205
  29.4 23.5 %collective-permute-start.1 = (bf16[1024,640]{1,0:T(8,128)(2,1)}, bf16[1024,640]{1,0:T(8,128)(2,1)}, u32[]{:S(2)}, u32[]{:S(2)}) collective-permute-start(bf16[1024,640]{1,0:T(8,128)(2,1)} %get-tuple-element.41), channel_id=1, source_target_pairs={{0,4},{4,0},{8,20},{12,16},{16,12},{20,8},{24,28},{28,24},{1,5},{5... | collective-permute-start | bytes 3932168 | tf_op jit(solution)/shard_map/ppermute | solution.py:205
  30.0 36.3 %copy-start.6 = (bf16[4,16,4096]{2,1,0:T(8,128)(2,1)}, bf16[4,16,4096]{2,1,0:T(8,128)(2,1)S(1)}, u32[]{:S(2)}) copy-start(bf16[4,16,4096]{2,1,0:T(8,128)(2,1)S(1)} %all-to-all-done.1) | copy-start | bytes 1572868
  30.0 18.4 %collective-permute-start.2 = (bf16[64,4096]{1,0:T(8,128)(2,1)S(1)}, bf16[64,4096]{1,0:T(8,128)(2,1)}, u32[]{:S(2)}, u32[]{:S(2)}) collective-permute-start(bf16[64,4096]{1,0:T(8,128)(2,1)S(1)} %bitcast.13), channel_id=1, source_target_pairs={{0,32},{32,64},{64,96},{96,128},{128,160},{160,192},{192,224},{224... | collective-permute-start | bytes 1572872 | tf_op jit(solution)/shard_map/ppermute | solution.py:256
  31.9 16.5 %collective-permute-start.4 = (bf16[64,4096]{1,0:T(8,128)(2,1)S(1)}, bf16[64,4096]{1,0:T(8,128)(2,1)}, u32[]{:S(2)}, u32[]{:S(2)}) collective-permute-start(bf16[64,4096]{1,0:T(8,128)(2,1)S(1)} %bitcast.14), channel_id=1, source_target_pairs={{0,224},{32,0},{64,32},{96,64},{128,96},{160,128},{192,160},{224,1... | collective-permute-start | bytes 1572872 | tf_op jit(solution)/shard_map/ppermute | solution.py:256
  48.4 10.7 %collective-permute-start.3 = (bf16[64,4096]{1,0:T(8,128)(2,1)}, bf16[64,4096]{1,0:T(8,128)(2,1)}, u32[]{:S(2)}, u32[]{:S(2)}) collective-permute-start(bf16[64,4096]{1,0:T(8,128)(2,1)} %collective-permute-done.2.refs_4_), channel_id=1, source_target_pairs={{0,32},{32,64},{64,96},{96,128},{128,160},{160,192},{192,224},{224... | collective-permute-start | bytes 1572872 | tf_op jit(solution)/shard_map/ppermute | solution.py:256
  48.4 10.7 %collective-permute-start.5 = (bf16[64,4096]{1,0:T(8,128)(2,1)}, bf16[64,4096]{1,0:T(8,128)(2,1)}, u32[]{:S(2)}, u32[]{:S(2)}) collective-permute-start(bf16[64,4096]{1,0:T(8,128)(2,1)} %collective-permute-done.4.refs_1_), channel_id=1, source_target_pairs={{0,224},{32,0},{64,32},{96,64},{128,96},{160,128},{192,160},{224,1... | collective-permute-start | bytes 1572872 | tf_op jit(solution)/shard_map/ppermute | solution.py:256
  59.1 5.0 %collective-permute-start.6 = (bf16[1024,640]{1,0:T(8,128)(2,1)}, bf16[1024,640]{1,0:T(8,128)(2,1)}, u32[]{:S(2)}, u32[]{:S(2)}) collective-permute-start(bf16[1024,640]{1,0:T(8,128)(2,1)} %collective-permute-done.refs_5_), channel_id=1, source_target_pairs={{0,16},{16,0},{1,17},{17,1},{2,18},{18,2},{3,19},{19,3},{4,20},{20... | collective-permute-start | bytes 3932168 | tf_op jit(solution)/shard_map/ppermute | solution.py:247
  59.1 7.1 %collective-permute-start.7 = (bf16[1024,640]{1,0:T(8,128)(2,1)}, bf16[1024,640]{1,0:T(8,128)(2,1)}, u32[]{:S(2)}, u32[]{:S(2)}) collective-permute-start(bf16[1024,640]{1,0:T(8,128)(2,1)} %collective-permute-done.1.refs_6_), channel_id=1, source_target_pairs={{0,16},{16,0},{1,17},{17,1},{2,18},{18,2},{3,19},{19,3},{4,20},{20... | collective-permute-start | bytes 3932168 | tf_op jit(solution)/shard_map/ppermute | solution.py:247
  59.6 69.9 %collective-permute-start.20 = (bf16[1024,1280]{1,0:T(8,128)(2,1)S(1)}, bf16[1024,1280]{1,0:T(8,128)(2,1)}, u32[]{:S(2)}, u32[]{:S(2)}) collective-permute-start(bf16[1024,1280]{1,0:T(8,128)(2,1)S(1)} %copy-done), channel_id=1, source_target_pairs={{0,16},{16,0},{1,17},{17,1},{2,18},{18,2},{3,19},{19,3},{4,20},{20... | collective-permute-start | bytes 7864328 | tf_op jit(solution)/shard_map/ppermute | solution.py:248
  59.6 16.4 %collective-permute-start.8 = (bf16[64,4096]{1,0:T(8,128)(2,1)}, bf16[64,4096]{1,0:T(8,128)(2,1)}, u32[]{:S(2)}, u32[]{:S(2)}) collective-permute-start(bf16[64,4096]{1,0:T(8,128)(2,1)} %collective-permute-done.3.refs_3_), channel_id=1, source_target_pairs={{0,32},{32,64},{64,96},{96,128},{128,160},{160,192},{192,224},{224... | collective-permute-start | bytes 1572872 | tf_op jit(solution)/shard_map/ppermute | solution.py:256
  59.6 16.4 %collective-permute-start.9 = (bf16[64,4096]{1,0:T(8,128)(2,1)}, bf16[64,4096]{1,0:T(8,128)(2,1)}, u32[]{:S(2)}, u32[]{:S(2)}) collective-permute-start(bf16[64,4096]{1,0:T(8,128)(2,1)} %collective-permute-done.5.refs_2_), channel_id=1, source_target_pairs={{0,224},{32,0},{64,32},{96,64},{128,96},{160,128},{192,160},{224,1... | collective-permute-start | bytes 1572872 | tf_op jit(solution)/shard_map/ppermute | solution.py:256
  77.0 11.6 %collective-permute-start.10 = (bf16[32,4096]{1,0:T(8,128)(2,1)S(1)}, bf16[32,4096]{1,0:T(8,128)(2,1)S(1)}, u32[]{:S(2)}, u32[]{:S(2)}) collective-permute-start(bf16[32,4096]{1,0:T(8,128)(2,1)S(1)} %slice.15), channel_id=1, source_target_pairs={{0,32},{32,64},{64,96},{96,128},{128,160},{160,192},{192,224},{224... | collective-permute-start | bytes 786440 | tf_op jit(solution)/shard_map/ppermute | solution.py:256
  80.7 7.9 %collective-permute-start.11 = (bf16[32,4096]{1,0:T(8,128)(2,1)S(1)}, bf16[32,4096]{1,0:T(8,128)(2,1)S(1)}, u32[]{:S(2)}, u32[]{:S(2)}) collective-permute-start(bf16[32,4096]{1,0:T(8,128)(2,1)S(1)} %slice.16), channel_id=1, source_target_pairs={{0,224},{32,0},{64,32},{96,64},{128,96},{160,128},{192,160},{224,1... | collective-permute-start | bytes 786440 | tf_op jit(solution)/shard_map/ppermute | solution.py:256
  88.6 0.7 copy-start.7
  88.6 0.7 copy-start.8
  96.0 23.3 %copy-start.3 = (s32[4]{0:T(128)S(1)}, s32[4]{0:T(128)}, u32[]{:S(2)}) copy-start(s32[4]{0:T(128)} %pad_add_fusion.pos) | copy-start | bytes 52
  96.0 33.5 %copy-start.1 = (s32[512,1]{1,0:T(8,128)S(1)}, s32[512,1]{1,0:T(8,128)}, u32[]{:S(2)}) copy-start(s32[512,1]{1,0:T(8,128)} %copy.20.targets) | copy-start | bytes 6148
  96.0 17.5 %collective-permute-start.16 = (bf16[512,640]{1,0:T(8,128)(2,1)}, bf16[512,640]{1,0:T(8,128)(2,1)S(1)}, u32[]{:S(2)}, u32[]{:S(2)}) collective-permute-start(bf16[512,640]{1,0:T(8,128)(2,1)} %get-tuple-element.64.e0), channel_id=1, source_target_pairs={{0,4},{4,8},{8,12},{12,0},{1,5},{5,9},{9,13},{13,1},{2,6},{6,10},{... | collective-permute-start | bytes 1966088 | tf_op jit(solution)/shard_map/ppermute | solution.py:262
  97.4 17.0 %collective-permute-start.18 = (bf16[512,640]{1,0:T(8,128)(2,1)}, bf16[512,640]{1,0:T(8,128)(2,1)}, u32[]{:S(2)}, u32[]{:S(2)}) collective-permute-start(bf16[512,640]{1,0:T(8,128)(2,1)} %get-tuple-element.64.e0), channel_id=1, source_target_pairs={{0,12},{4,0},{8,4},{12,8},{1,13},{5,1},{9,5},{13,9},{2,14},{6,2},{... | collective-permute-start | bytes 1966088 | tf_op jit(solution)/shard_map/ppermute | solution.py:262
  99.3 19.9 %all-to-all-start.2 = ((f32[32,16,128]{2,1,0:T(8,128)}), f32[32,16,128]{2,1,0:T(8,128)}, u32[]{:S(2)}, u32[]{:S(2)}) async-start(f32[32,16,128]{2,1,0:T(8,128)} %get-tuple-element.60), calls=%async_computation.2 | async-start | bytes 524288 | tf_op jit(solution)/shard_map/all_to_all | solution.py:263
  114.2 15.2 %collective-permute-start.17 = (bf16[256,640]{1,0:T(8,128)(2,1)}, bf16[256,640]{1,0:T(8,128)(2,1)}, u32[]{:S(2)}, u32[]{:S(2)}) collective-permute-start(bf16[256,640]{1,0:T(8,128)(2,1)} %slice.20), channel_id=1, source_target_pairs={{0,4},{4,8},{8,12},{12,0},{1,5},{5,9},{9,13},{13,1},{2,6},{6,10},{... | collective-permute-start | bytes 983048 | tf_op jit(solution)/shard_map/ppermute | solution.py:264
  116.1 13.4 %collective-permute-start.19 = (bf16[256,640]{1,0:T(8,128)(2,1)}, bf16[256,640]{1,0:T(8,128)(2,1)}, u32[]{:S(2)}, u32[]{:S(2)}) collective-permute-start(bf16[256,640]{1,0:T(8,128)(2,1)} %slice.21), channel_id=1, source_target_pairs={{0,12},{4,0},{8,4},{12,8},{1,13},{5,1},{9,5},{13,9},{2,14},{6,2},{... | collective-permute-start | bytes 983048 | tf_op jit(solution)/shard_map/ppermute | solution.py:265
  120.3 4.9 %collective-permute-start.12 = (f32[16,128]{1,0:T(8,128)S(1)}, f32[16,128]{1,0:T(8,128)S(1)}, u32[]{:S(2)}, u32[]{:S(2)}) collective-permute-start(f32[16,128]{1,0:T(8,128)S(1)} %shard_map.70.t0), channel_id=1, source_target_pairs={{0,4},{4,8},{8,12},{12,0},{1,5},{5,9},{9,13},{13,1},{2,6},{6,10},{... | collective-permute-start | bytes 24584 | tf_op jit(solution)/shard_map/ppermute | solution.py:267
  120.4 5.2 %collective-permute-start.13 = (f32[16,128]{1,0:T(8,128)S(1)}, f32[16,128]{1,0:T(8,128)S(1)}, u32[]{:S(2)}, u32[]{:S(2)}) collective-permute-start(f32[16,128]{1,0:T(8,128)S(1)} %shard_map.70.t0), channel_id=1, source_target_pairs={{0,8},{4,12},{8,0},{12,4},{1,9},{5,13},{9,1},{13,5},{2,10},{6,14},... | collective-permute-start | bytes 24584 | tf_op jit(solution)/shard_map/ppermute | solution.py:267
  125.2 3.7 %collective-permute-start.14 = (f32[16,128]{1,0:T(8,128)S(1)}, f32[16,128]{1,0:T(8,128)S(1)}, u32[]{:S(2)}, u32[]{:S(2)}) collective-permute-start(f32[16,128]{1,0:T(8,128)S(1)} %shard_map.70.t0), channel_id=1, source_target_pairs={{0,12},{4,0},{8,4},{12,8},{1,13},{5,1},{9,5},{13,9},{2,14},{6,2},{... | collective-permute-start | bytes 24584 | tf_op jit(solution)/shard_map/ppermute | solution.py:267
  129.5 8.0 %copy-start.4 = (f32[8,512]{1,0:T(8,128)}, f32[8,512]{1,0:T(8,128)S(1)}, u32[]{:S(2)}) copy-start(f32[8,512]{1,0:T(8,128)S(1)} %get-tuple-element.62) | copy-start | bytes 49156
  129.5 1.1 copy-start.2
  130.6 7.2 %copy-start.5 = (bf16[512,1024]{1,0:T(8,128)(2,1)S(1)}, bf16[512,1024]{1,0:T(8,128)(2,1)}, u32[]{:S(2)}) copy-start(bf16[512,1024]{1,0:T(8,128)(2,1)} %get-tuple-element.67.h0) | copy-start | bytes 3145732
  137.4 4.8 %collective-permute-start.22 = (bf16[512,1280]{1,0:T(8,128)(2,1)S(1)}, bf16[512,1280]{1,0:T(8,128)(2,1)S(1)}, u32[]{:S(2)}, u32[]{:S(2)}) collective-permute-start(bf16[512,1280]{1,0:T(8,128)(2,1)S(1)} %get-tuple-element.69), channel_id=1, source_target_pairs={{0,16},{16,0},{1,17},{17,1},{2,18},{18,2},{3,19},{19,3},{4,20},{20... | collective-permute-start | bytes 3932168 | tf_op jit(solution)/shard_map/ppermute | solution.py:281
  137.8 4.5 %collective-permute-start.21 = (bf16[512,1024]{1,0:T(8,128)(2,1)S(1)}, bf16[512,1024]{1,0:T(8,128)(2,1)S(1)}, u32[]{:S(2)}, u32[]{:S(2)}) collective-permute-start(bf16[512,1024]{1,0:T(8,128)(2,1)S(1)} %copy-done.5), channel_id=1, source_target_pairs={{0,16},{16,0},{1,17},{17,1},{2,18},{18,2},{3,19},{19,3},{4,20},{20... | collective-permute-start | bytes 3145736 | tf_op jit(solution)/shard_map/ppermute | solution.py:269
  138.2 9.2 %collective-permute-start.23 = (bf16[8,16,1024]{2,1,0:T(8,128)(2,1)S(1)}, bf16[8,16,1024]{2,1,0:T(8,128)(2,1)S(1)}, u32[]{:S(2)}, u32[]{:S(2)}) collective-permute-start(bf16[8,16,1024]{2,1,0:T(8,128)(2,1)S(1)} %get-tuple-element.70), channel_id=1, source_target_pairs={{0,1},{1,2},{2,3},{3,0},{4,5},{5,6},{6,7},{7,4},{8,9},{9,10},{10,1... | collective-permute-start | bytes 786440 | tf_op jit(solution)/shard_map/ppermute | solution.py:280
  139.8 10.7 %collective-permute-start.24 = (bf16[8,16,1024]{2,1,0:T(8,128)(2,1)S(1)}, bf16[8,16,1024]{2,1,0:T(8,128)(2,1)S(1)}, u32[]{:S(2)}, u32[]{:S(2)}) collective-permute-start(bf16[8,16,1024]{2,1,0:T(8,128)(2,1)S(1)} %get-tuple-element.71), channel_id=1, source_target_pairs={{0,2},{1,3},{2,0},{3,1},{4,6},{5,7},{6,4},{7,5},{8,10},{9,11},{10,... | collective-permute-start | bytes 786440 | tf_op jit(solution)/shard_map/ppermute | solution.py:280
  141.2 13.7 %collective-permute-start.25 = (bf16[8,16,1024]{2,1,0:T(8,128)(2,1)S(1)}, bf16[8,16,1024]{2,1,0:T(8,128)(2,1)S(1)}, u32[]{:S(2)}, u32[]{:S(2)}) collective-permute-start(bf16[8,16,1024]{2,1,0:T(8,128)(2,1)S(1)} %get-tuple-element.72), channel_id=1, source_target_pairs={{0,3},{1,0},{2,1},{3,2},{4,7},{5,4},{6,5},{7,6},{8,11},{9,8},{10,9... | collective-permute-start | bytes 786440 | tf_op jit(solution)/shard_map/ppermute | solution.py:280
  155.8 16.6 %all-to-all-start.3 = ((bf16[8,16,1024]{2,1,0:T(8,128)(2,1)}), bf16[8,16,1024]{2,1,0:T(8,128)(2,1)S(1)}, u32[]{:S(2)}, u32[]{:S(2)}) async-start(bf16[8,16,1024]{2,1,0:T(8,128)(2,1)} %add_convert_fusion), calls=%async_computation.3 | async-start | bytes 524288 | tf_op jit(solution)/shard_map/all_to_all | solution.py:294
  161.1 1.2 collective-permute-start.15
